TPU v7x, 128 devices: a whole 4x4x4 slice. The times are simulated.
128 devices in a mesh: store: 8 (over x, core), ep: 16 (over y, z).
Axes of the slice: x: 4, y: 4, z: 4, core: 2. Of those that a mesh axis runs over, the one named last changes fastest.
Arguments:
- queries: bfloat16 [1024, 36864], P('store', 'ep'), may hold values from -30 to 30
- residual_in: bfloat16 [1024, 7168], P(('store', 'ep')), may hold values from -6 to 6
- latent_store: bfloat16 [256, 128, 576], P('store'), may hold values from -5 to 5
- group_passages: int32 [256], replicated, may hold values from 0 to 255, as said below
- row_slots: int32 [1024, 16], P('store'), may hold values from 0 to 31, as said below
- passage_place: int32 [256], replicated, may hold values from 0 to 255, as said below
- w_uv: bfloat16 [64, 512, 128], P('ep'), may hold values from -0.25 to 0.25
- w_out: bfloat16 [8192, 7168], P('ep'), may hold values from -0.5 to 0.5
- expert_ids: int32 [1024, 4], P(('store', 'ep')), may hold values from 0 to 15, all different within a row; in each aligned block of 8 rows (0 to 7, 8 to 15, ...) at most 4 rows name the same one
- expert_gates: float32 [1024, 4], P(('store', 'ep')), may hold values from 0.2 to 1.2
- w_gate: bfloat16 [16, 7168, 2048], P('ep', None, 'store'), may hold values from -0.0625 to 0.0625
- w_up: bfloat16 [16, 7168, 2048], P('ep', None, 'store'), may hold values from -0.0625 to 0.0625
- w_down: bfloat16 [16, 2048, 7168], P('ep', 'store'), may hold values from -0.125 to 0.125
Outputs:
- layer_out: bfloat16 [1024, 7168], P(('store', 'ep'))
Inputs may be any that keep to these rules, and one draw needn't show every extreme that they name: A permutation: passage p lies in row passage_place[p] of latent_store. `group_passages`: the 32 passages of one group are distinct, and slot i of every group's list names a passage held by store shard i // 4, that is with passage_place in [(i // 4) * 32, (i // 4 + 1) * 32). `row_slots`: each row names 16 distinct slots. `expert_ids`: each row names 4 different experts; among the rows of one device no expert is named by more than 4 rows.
All inputs are finite; a program needn't handle non-finite values.
Results may differ from a plain program's by a relative error of at most 0.022.
Values may be sent and summed in bfloat16 or wider, within the bound.
A program may use at most 128 MiB of HBM per device.

v0:
```python
import jax
import jax.numpy as jnp
from jax import lax
from jax.sharding import PartitionSpec as P

score_scale = 192.0 ** (-0.5)


def build_slots(chosen_ids, expert_count, capacity):
    expert_range = jnp.arange(expert_count, dtype=jnp.int32)
    routed = jnp.sum((chosen_ids[..., None] == expert_range).astype(jnp.int32), axis=-2)
    earlier = jnp.cumsum(routed, axis=-2) - routed
    depth_range = jnp.arange(capacity, dtype=jnp.int32)
    slot_mask = (routed[..., None] == 1) & (earlier[..., None] == depth_range)
    return jnp.moveaxis(slot_mask, -3, -1)


def body(
    queries,
    residual_in,
    latent_store,
    group_passages,
    row_slots,
    passage_place,
    w_uv,
    w_out,
    expert_ids,
    expert_gates,
    w_gate,
    w_up,
    w_down,
):
    store_count = lax.axis_size("store")
    store_index = lax.axis_index("store")
    expert_count = lax.axis_size("ep")
    shard_len, block_len, latent_width = latent_store.shape
    value_width = w_uv.shape[1]
    heads_here = w_uv.shape[0]
    group_rows = queries.shape[0]
    slot_count = group_passages.shape[0] // store_count
    per_shard = slot_count // store_count
    group_lists = group_passages.reshape(store_count, store_count, per_shard)
    own_lists = lax.dynamic_index_in_dim(group_lists, store_index, 1, keepdims=False)
    local_rows = passage_place[own_lists] - store_index * shard_len
    served = latent_store[local_rows]
    fetched = lax.all_to_all(served, "store", split_axis=0, concat_axis=0, tiled=True)
    key_rows = fetched.reshape(slot_count * block_len, latent_width)
    query_heads = queries.reshape(group_rows, heads_here, latent_width)
    chosen = jnp.any(row_slots[:, :, None] == jnp.arange(slot_count, dtype=jnp.int32), axis=1)
    kept_mask = jnp.repeat(chosen, block_len, axis=1)[:, None, :]
    scores = (
        jnp.einsum("rhc,tc->rht", query_heads, key_rows, preferred_element_type=jnp.float32)
        * score_scale
    )
    row_max = jnp.max(jnp.where(kept_mask, scores, -jnp.inf), axis=2, keepdims=True)
    exponent = jnp.where(kept_mask, jnp.exp(scores - row_max), 0.0)
    weights = (exponent / jnp.sum(exponent, axis=2, keepdims=True)).astype(jnp.bfloat16)
    latent_out = jnp.einsum(
        "rht,tc->rhc", weights, key_rows[:, :value_width], preferred_element_type=jnp.float32
    ).astype(jnp.bfloat16)
    head_out = jnp.einsum(
        "rhc,hcv->rhv", latent_out, w_uv, preferred_element_type=jnp.float32
    ).astype(jnp.bfloat16)
    head_out = head_out.reshape(group_rows, heads_here * w_uv.shape[2])
    tok_rows, model_width = residual_in.shape
    row_block = head_out
    attended = lax.psum_scatter(
        jnp.dot(row_block, w_out, preferred_element_type=jnp.float32).astype(jnp.bfloat16),
        "ep",
        scatter_dimension=0,
        tiled=True,
    ).astype(jnp.float32)
    mixed_rows = residual_in.astype(jnp.float32) + attended
    normed = (
        mixed_rows * lax.rsqrt(jnp.mean(mixed_rows * mixed_rows, axis=1, keepdims=True) + 1e-06)
    ).astype(jnp.bfloat16)
    top_count = expert_ids.shape[1]
    capacity = min(tok_rows, 2 * ((tok_rows * top_count + expert_count - 1) // expert_count))
    slot_table = build_slots(expert_ids, expert_count, capacity).astype(jnp.bfloat16)
    outgoing = jnp.einsum(
        "ecr,rd->ecd", slot_table, normed, preferred_element_type=jnp.float32
    ).astype(jnp.bfloat16)
    arrived = lax.all_to_all(outgoing, "ep", split_axis=0, concat_axis=0, tiled=True)
    gathered = lax.all_gather(
        arrived.reshape(expert_count * capacity, model_width), "store", axis=0, tiled=True
    )
    row_block = gathered
    gate_proj = jnp.dot(row_block, w_gate[0], preferred_element_type=jnp.float32)
    up_proj = jnp.dot(row_block, w_up[0], preferred_element_type=jnp.float32)
    hidden = (jax.nn.silu(gate_proj) * up_proj).astype(jnp.bfloat16)
    summed = lax.psum_scatter(
        jnp.dot(hidden, w_down[0], preferred_element_type=jnp.float32).astype(jnp.bfloat16),
        "store",
        scatter_dimension=0,
        tiled=True,
    )
    expert_rows = summed.reshape(expert_count, capacity, model_width)
    returned = lax.all_to_all(expert_rows, "ep", split_axis=0, concat_axis=0, tiled=True)
    expert_range = jnp.arange(expert_count, dtype=jnp.int32)
    gate_of = jnp.sum(
        jnp.where(expert_ids[:, :, None] == expert_range, expert_gates[:, :, None], 0.0), axis=1
    )
    weighted = slot_table.astype(jnp.float32) * jnp.transpose(gate_of)[:, None, :]
    expert_mix = jnp.einsum(
        "ecr,ecd->rd", weighted, returned.astype(jnp.float32), precision=lax.Precision.HIGHEST
    )
    return (mixed_rows + expert_mix).astype(jnp.bfloat16)


def solution(mesh):
    return jax.shard_map(
        body,
        mesh=mesh,
        in_specs=(
            P("store", "ep"),
            P(("store", "ep"), None),
            P("store", None, None),
            P(),
            P("store", None),
            P(),
            P("ep", None, None),
            P("ep", None),
            P(("store", "ep"), None),
            P(("store", "ep"), None),
            P("ep", None, "store"),
            P("ep", None, "store"),
            P("ep", "store", None),
        ),
        out_specs=P(("store", "ep"), None),
        check_vma=False,
    )
```

profile of v0, /device:TPU:1, one launch (start us, length us, event | category | flops | bytes accessed | tf_op | source)
XLA Modules:
  0.0 394.6 jit_solution(11536306133681497348)
XLA Ops:
  7.7 1.4 gather_fusion
  9.4 5.7 %gather_fusion.1 = bf16[32,128,576]{1,2,0:T(8,128)(2,1)} fusion(bf16[32,128,576]{1,2,0:T(8,128)(2,1)} %param.15, s32[1024]{0:T(1024)S(1)} %pad_clamp_fusion), kind=kCustom, calls=%fused_computation.1 | custom fusion | bytes 9437312 | tf_op jit(solution)/shard_map/gather | solution.py:45
  15.1 8.1 %copy.79 = bf16[8,4,128,576]{2,1,3,0:T(4,128)(2,1)} copy(bf16[8,4,128,576]{2,3,1,0:T(8,128)(2,1)} %bitcast.78) | data formatting | bytes 9437184 | tf_op jit(solution)/shard_map/gather | solution.py:45
  23.2 6.0 %all-to-all-start = ((bf16[8,4,128,576]{2,1,3,0:T(4,128)(2,1)}), bf16[8,4,128,576]{2,1,3,0:T(4,128)(2,1)}, u32[]{:S(2)}, u32[]{:S(2)}) async-start(bf16[8,4,128,576]{2,1,3,0:T(4,128)(2,1)} %copy.79), calls=%async_computation | async-start | bytes 9437184 | tf_op jit(solution)/shard_map/all_to_all | solution.py:46
  29.6 54.2 %all-to-all-done = bf16[8,4,128,576]{2,1,3,0:T(4,128)(2,1)} async-done(((bf16[8,4,128,576]{2,1,3,0:T(4,128)(2,1)}), bf16[8,4,128,576]{2,1,3,0:T(4,128)(2,1)}, u32[]{:S(2)}, u32[]{:S(2)}) %all-to-all-start) | async-done | bytes 4718624 | tf_op jit(solution)/shard_map/all_to_all | solution.py:46
  83.8 6.1 %copy.80 = bf16[8,4,128,576]{2,1,0,3:T(4,128)(2,1)} copy(bf16[8,4,128,576]{2,1,3,0:T(4,128)(2,1)} %all-to-all-done) | data formatting | bytes 9437184 | tf_op jit(solution)/shard_map/all_to_all | solution.py:46
  89.9 8.8 %reshape.119 = bf16[4096,576,1]{0,1,2:T(8,128)(2,1)} reshape(bf16[8,4,128,576]{2,1,0,3:T(4,128)(2,1)} %copy.80) | data formatting | bytes 9437184 | tf_op jit(solution)/shard_map/reshape | solution.py:47
  98.7 8.8 %reshape.93 = bf16[4096,576]{0,1:T(8,128)(2,1)} reshape(bf16[8,4,128,576]{2,1,0,3:T(4,128)(2,1)} %copy.80) | data formatting | bytes 9437184 | tf_op jit(solution)/shard_map/reshape | solution.py:47
  107.6 15.4 %fusion.49 = (f32[128,4]{0,1:T(4,128)S(1)}, f32[128,4,4096]{0,2,1:T(8,128)}) fusion(pred[128,4096]{0,1:T(8,128)(4,1)S(1)} %bitcast.80, bf16[4096,576,1]{0,1,2:T(8,128)(2,1)} %reshape.119, bf16[128,4,576]{0,2,1:T(8,128)(2,1)S(1)} %bitcast.79), kind=kOutput, calls=%fused_computation.67 | convolution fusion | flops 4844425216 | bytes 14223360 | tf_op jit(solution)/shard_map/sub | solution.py:56
  123.0 7.1 %fusion.24 = bf16[4,128,128]{1,2,0:T(8,128)(2,1)S(1)} fusion(bf16[4,512,128]{2,1,0:T(8,128)(2,1)S(1)} %copy-done, bf16[4096,576]{0,1:T(8,128)(2,1)} %reshape.93, f32[128,4,4096]{0,2,1:T(8,128)} %get-tuple-element.6, f32[128,4]{0,1:T(4,128)S(1)} %get-tuple-element.5), kind=kOutput, calls=%fused_computation.30 | convolution fusion | flops 2219114496 | bytes 13240320 | tf_op jit(solution)/shard_map/rhc,hcv->rhv/dot_general | solution.py:61
  130.2 5.5 %convolution_convert_fusion.1 = bf16[128,7168]{1,0:T(8,128)(2,1)} fusion(bf16[128,512]{0,1:T(8,128)(2,1)S(1)} %bitcast.81, bf16[512,7168]{1,0:T(8,128)(2,1)} %param.20), kind=kOutput, calls=%fused_computation.4 | convolution fusion | flops 940441600 | bytes 9306112 | tf_op jit(solution)/shard_map/dot_general | solution.py:68
  137.4 87.7 %all-reduce.3.cloned.1.call-done = bf16[128,7168]{1,0:T(8,128)(2,1)} async-done(((bf16[128,7168]{1,0:T(8,128)(2,1)}), bf16[128,7168]{1,0:T(8,128)(2,1)}) %all-reduce.3.cloned.1.call-update) | async-done | bytes 1835024
  225.1 1.1 multiply_reduce_fusion
  226.2 1.4 convolution_convert_fusion.2
  228.3 17.3 %all_to_all.15 = bf16[16,4,7168]{2,1,0:T(4,128)(2,1)S(1)} all-to-all(bf16[16,4,7168]{2,1,0:T(4,128)(2,1)S(1)} %copy.85), channel_id=1, replica_groups=mesh['store'=8,'ep'=16] {'ep'}, dimensions={0} | all-to-all | bytes 1835008 | tf_op jit(solution)/shard_map/all_to_all | solution.py:83
  245.5 1.1 reshape.96
  246.7 46.6 %all-gather.2.cloned.1.call-done = bf16[512,7168]{1,0:T(8,128)(2,1)} async-done(((bf16[64,7168]{1,0:T(8,128)(2,1)}), bf16[512,7168]{1,0:T(8,128)(2,1)}) %all-gather.2.cloned.1.call-update) | async-done | bytes 7340048 | tf_op jit(solution)/shard_map/all_gather | solution.py:84
  293.4 6.2 %fusion.14 = f32[512,256]{1,0:T(8,128)S(1)} fusion(bf16[512,7168]{1,0:T(8,128)(2,1)} %all-gather.2.cloned.1.call-done, bf16[1,7168,256]{2,1,0:T(8,128)(2,1)} %param.23), kind=kOutput, calls=%fused_computation.24 | convolution fusion | flops 1879048192 | bytes 11534336 | tf_op jit(solution)/shard_map/dot_general | solution.py:88
  299.6 16.0 %convolution_convert_fusion = bf16[512,7168]{1,0:T(8,128)(2,1)} fusion(bf16[1,256,7168]{2,1,0:T(8,128)(2,1)} %param.25, bf16[512,7168]{1,0:T(8,128)(2,1)} %all-gather.2.cloned.1.call-done, bf16[1,7168,256]{2,1,0:T(8,128)(2,1)} %param.24, f32[512,256]{1,0:T(8,128)S(1)} %fusion.14), kind=kOutput, calls=%fused_computation.3 | convolution fusion | flops 3762552832 | bytes 22544384 | tf_op jit(solution)/shard_map/dot_general | solution.py:92
  315.6 46.7 %reduce-scatter.2.cloned.1.call-done = bf16[64,7168]{1,0:T(8,128)(2,1)} async-done(((bf16[512,7168]{1,0:T(8,128)(2,1)}), bf16[64,7168]{1,0:T(8,128)(2,1)}) %reduce-scatter.2.cloned.1.call-update) | async-done | bytes 917520 | tf_op jit(solution)/shard_map/reduce_scatter | solution.py:91
  362.3 2.5 reshape.97
  364.9 6.7 %all-to-all-start.2 = ((bf16[16,4,7168]{2,1,0:T(4,128)(2,1)}), bf16[16,4,7168]{2,1,0:T(4,128)(2,1)S(1)}, u32[]{:S(2)}, u32[]{:S(2)}) async-start(bf16[16,4,7168]{2,1,0:T(4,128)(2,1)} %reshape.97), calls=%async_computation.3 | async-start | bytes 1835008 | tf_op jit(solution)/shard_map/all_to_all | solution.py:98
  371.7 13.8 %all-to-all-done.2 = bf16[16,4,7168]{2,1,0:T(4,128)(2,1)S(1)} async-done(((bf16[16,4,7168]{2,1,0:T(4,128)(2,1)}), bf16[16,4,7168]{2,1,0:T(4,128)(2,1)S(1)}, u32[]{:S(2)}, u32[]{:S(2)}) %all-to-all-start.2) | async-done | bytes 917536 | tf_op jit(solution)/shard_map/all_to_all | solution.py:98
  385.4 2.6 fusion.5
  (47 shorter events, 3.8 us)
Async XLA Ops:
  6.5 116.5 %copy-start = (bf16[4,512,128]{2,1,0:T(8,128)(2,1)S(1)}, bf16[4,512,128]{2,1,0:T(8,128)(2,1)}, u32[]{:S(2)}) copy-start(bf16[4,512,128]{2,1,0:T(8,128)(2,1)} %param.19) | copy-start | bytes 1572868
  23.2 6.1 %copy-start.2 = (bf16[128,2304]{1,0:T(8,128)(2,1)S(1)}, bf16[128,2304]{1,0:T(8,128)(2,1)}, u32[]{:S(2)}) copy-start(bf16[128,2304]{1,0:T(8,128)(2,1)} %param.13) | copy-start | bytes 1769476
  23.2 6.4 %copy-start.4 = (s32[128,16]{0,1:T(8,128)S(1)}, s32[128,16]{0,1:T(8,128)}, u32[]{:S(2)}) copy-start(s32[128,16]{0,1:T(8,128)} %param.17) | copy-start | bytes 24580
  23.2 60.6 %all-to-all-start = ((bf16[8,4,128,576]{2,1,3,0:T(4,128)(2,1)}), bf16[8,4,128,576]{2,1,3,0:T(4,128)(2,1)}, u32[]{:S(2)}, u32[]{:S(2)}) async-start(bf16[8,4,128,576]{2,1,3,0:T(4,128)(2,1)} %copy.79), calls=%async_computation | async-start | bytes 9437184 | tf_op jit(solution)/shard_map/all_to_all | solution.py:46
  29.2 195.9 %all-reduce.3.cloned.1.call-start = ((), (), s32[]{:S(2)}) async-start(), calls=%async_computation.6 | async-start | bytes 3670016
  130.2 5.9 %copy-start.5 = (s32[8,4]{0,1:T(4,128)S(1)}, s32[8,4]{0,1:T(4,128)}, u32[]{:S(2)}) copy-start(s32[8,4]{0,1:T(4,128)} %param.21) | copy-start | bytes 388
  130.2 6.0 %copy-start.7 = (u32[128]{0:T(128)S(1)}, u32[128]{0:T(128)}, u32[]{:S(2)}) copy-start(u32[128]{0:T(128)} %constant.49) | copy-start | bytes 1540
  130.2 94.9 %copy-start.3 = (bf16[8,7168]{1,0:T(8,128)(2,1)S(1)}, bf16[8,7168]{1,0:T(8,128)(2,1)}, u32[]{:S(2)}) copy-start(bf16[8,7168]{1,0:T(8,128)(2,1)} %param.14) | copy-start | bytes 344068
  135.8 157.6 %all-gather.2.cloned.1.call-start = ((), (), s32[]{:S(2)}) async-start(), calls=%async_computation.4 | async-start | bytes 8257536 | tf_op jit(solution)/shard_map/all_gather | solution.py:84
  246.7 115.6 %reduce-scatter.2.cloned.1.call-start = ((), (), s32[]{:S(2)}) async-start(), calls=%async_computation.5 | async-start | bytes 8257536 | tf_op jit(solution)/shard_map/reduce_scatter | solution.py:91
  315.6 72.5 %copy-start.1 = (bf16[4,512,128]{2,1,0:T(8,128)(2,1)S(1)}, bf16[4,512,128]{2,1,0:T(8,128)(2,1)}, u32[]{:S(2)}) copy-start(bf16[4,512,128]{2,1,0:T(8,128)(2,1)} %param.19) | copy-start | bytes 1572868
  315.6 56.0 %copy-start.6 = (f32[8,4]{0,1:T(4,128)S(1)}, f32[8,4]{0,1:T(4,128)}, u32[]{:S(2)}) copy-start(f32[8,4]{0,1:T(4,128)} %param.22) | copy-start | bytes 388
  364.9 20.6 %all-to-all-start.2 = ((bf16[16,4,7168]{2,1,0:T(4,128)(2,1)}), bf16[16,4,7168]{2,1,0:T(4,128)(2,1)S(1)}, u32[]{:S(2)}, u32[]{:S(2)}) async-start(bf16[16,4,7168]{2,1,0:T(4,128)(2,1)} %reshape.97), calls=%async_computation.3 | async-start | bytes 1835008 | tf_op jit(solution)/shard_map/all_to_all | solution.py:98
Sparse Core Ops, SparseCore 0:
  135.9 89.1 all-reduce.2
  246.8 46.5 all-gather.1
  315.7 46.5 reduce-scatter.1
where the time goes:
time: 398 us; the launch traced here: 395 us
  waiting for transfers between devices  249 us (63%)
  matrix products  54.2 us (14%)
  local copies, waits for them, and re-layouts  45.7 us (11%)
  blocking collectives  17.3 us (4%)
  between operations  13.9 us (3%)
  starting transfers between devices  13 us (3%)
    unnamed x4, waiting for transfers between devices  87.7 us
    all_to_all x1, waiting for transfers between devices, body(): lax.all_to_all(served, 'store', split_axis=0, concat_axis=0, tiled=True)  54.2 us
    reduce_scatter x1, waiting for transfers between devices, body(): lax.psum_scatter(jnp.dot(hidden, w_down[0], preferred_element_type=jnp.fl...  46.7 us
    all_gather x1, waiting for transfers between devices, body(): lax.all_gather(arrived.reshape(expert_count * capacity, model_width), 'st...  46.6 us
    reshape x2, local copies, waits for them, and re-layouts, body(): key_rows = fetched.reshape(slot_count * block_len, latent_width)  17.6 us
    all_to_all x1, blocking collectives, body(): lax.all_to_all(outgoing, 'ep', split_axis=0, concat_axis=0, tiled=True)  17.3 us
    dot_general x1, matrix products, body(): jnp.dot(hidden, w_down[0], preferred_element_type=jnp.float32)  16 us
    sub x1, matrix products, body(): exponent = jnp.where(kept_mask, jnp.exp(scores - row_max), 0.0)  15.4 us
  transfers between devices with their start and end apart: 5, of which 5 were waited for; matrix products, arithmetic and copies ran while one was open for 0% of the time, Pallas kernels for 0%

commit v1 on v0

v1 whole, which is shorter than its diff:
```python
import functools

import jax
import jax.numpy as jnp
from jax import lax
from jax.experimental import pallas as pl
from jax.experimental.pallas import tpu as pltpu
from jax.sharding import PartitionSpec as P

score_scale = 192.0 ** (-0.5)
MESH = pl.DeviceIdType.MESH
LOW = -1e30


def offset_of(i):
    return i + i // 2 - 2 * (i // 3)


def attend_kernel(
    served, queries, chosen, w_uv, w_out, residual, w_down,
    mixed, normed, down_cols,
    kv, heads, mask, top, total, acc, head_out, out_w, part, part_in, summed, summed_in, rows,
    x_send, x_recv, g_send, g_recv, r_send, r_recv, d_send, d_recv, w_sem,
):
    s = lax.axis_index("store")
    e = lax.axis_index("ep")
    y, z = e // 4, e % 4

    def at_y(d):
        return (s, lax.rem(y + d, 4) * 4 + z)

    def at_z(d):
        return (s, y * 4 + lax.rem(z + d, 4))

    def at_s(d):
        return (lax.rem(s + d, 8), e)

    peers = [at_s(d) for d in range(1, 8)] + [at_y(d) for d in (1, 2, 3)] + [at_z(d) for d in (1, 2, 3)]
    barrier = pltpu.get_barrier_semaphore()
    for peer in peers:
        pl.semaphore_signal(barrier, inc=1, device_id=peer, device_id_type=MESH)
    get_w = pltpu.make_async_copy(w_out, out_w, w_sem.at[0])
    get_w.start()
    pl.semaphore_wait(barrier, len(peers))

    sent = []
    for d in range(1, 8):
        to = at_s(d)
        copy = pltpu.make_async_remote_copy(
            src_ref=served.at[to[0]],
            dst_ref=kv.at[e, pl.ds(pl.multiple_of(s * 32, 32), 32)],
            send_sem=x_send.at[d - 1], recv_sem=x_recv.at[d - 1],
            device_id=to, device_id_type=MESH,
        )
        copy.start()
        sent.append(copy)
    kv[e, pl.ds(pl.multiple_of(s * 32, 32), 32)] = served[s]

    for h in range(4):
        heads[h] = queries[:, h * 576:(h + 1) * 576]
    slot_row = lax.broadcasted_iota(jnp.int32, (32, 256), 0)
    token_col = lax.broadcasted_iota(jnp.int32, (32, 256), 1)
    for j in range(4):
        spread = (slot_row == (token_col // 32) * 4 + j).astype(jnp.bfloat16)
        mask[j] = jnp.dot(chosen[...], spread, preferred_element_type=jnp.float32)
    top[...] = jnp.full_like(top, LOW)
    total[...] = jnp.zeros_like(total)
    acc[...] = jnp.zeros_like(acc)

    def chunk(half, first, second):
        dy, dz = (first, second) if half == 0 else (second, first)
        return lax.rem(y - dy + 4, 4) * 4 + lax.rem(z - dz + 4, 4)

    def attend(p_a, p_b):
        keys = jnp.concatenate([kv[p_a, 0:128], kv[p_b, 128:256]], axis=0)
        live = jnp.concatenate([mask[p_a // 4][:, 0:128], mask[p_b // 4][:, 128:256]], axis=1)
        for h in range(4):
            scores = lax.dot_general(
                heads[h], keys, (((1,), (1,)), ((), ())), preferred_element_type=jnp.float32
            ) * score_scale
            scores = jnp.where(live > 0.5, scores, LOW)
            old = top[h]
            new = jnp.maximum(old, jnp.max(scores, axis=1, keepdims=True))
            exponent = jnp.exp(scores - new[:, 0:1]) * live
            scale = jnp.exp(old - new)
            top[h] = new
            total[h] = total[h] * scale + jnp.sum(exponent, axis=1, keepdims=True)
            acc[h] = acc[h] * scale[:, 0:1] + jnp.dot(
                exponent.astype(jnp.bfloat16), keys[:, 0:512], preferred_element_type=jnp.float32
            )

    def gather_copy(half, group, kind, place):
        low = half * 128 + (64 if kind == 3 else 0)
        size = 64 if kind >= 2 else 128
        on_y = (half == 0) == (group is None)
        to = (at_y if on_y else at_z)(1 if kind % 2 == 0 else 3)
        block = kv.at[place, pl.ds(low, size)]
        index = 4 if group is None else group
        return pltpu.make_async_remote_copy(
            src_ref=block, dst_ref=block,
            send_sem=g_send.at[half, index, kind], recv_sem=g_recv.at[half, index, kind],
            device_id=to, device_id_type=MESH,
        )

    def launch(group, offset):
        for half in (0, 1):
            for kind in (0, 1):
                gather_copy(half, group, kind, chunk(half, offset, 0)).start()

    for copy in sent:
        copy.wait_recv()
    launch(None, 0)
    launch(0, 0)
    attend(e, e)
    for kind in (0, 1):
        offset = 1 if kind == 0 else 3
        for half in (0, 1):
            gather_copy(half, None, kind, e).wait_recv()
            gather_copy(half, None, kind + 2, chunk(half, offset, 0)).start()
        launch(kind + 1, offset)

    def near(i, _):
        offset = 1 + 2 * i
        attend(chunk(0, offset, 0), chunk(1, offset, 0))
        return 0

    lax.fori_loop(0, 2, near, 0)
    for half in (0, 1):
        for kind in (2, 3):
            gather_copy(half, None, kind, e).wait_recv()
    launch(3, 2)
    attend(chunk(0, 2, 0), chunk(1, 2, 0))

    def sides(i, _):
        offset = offset_of(i)
        for kind in (0, 1):
            back = 1 if kind == 0 else 3
            for half in (0, 1):
                gather_copy(half, i, kind, e).wait_recv()
                gather_copy(half, i, kind + 2, chunk(half, offset, back)).start()

        def both(k, _):
            attend(chunk(0, offset, 1 + 2 * k), chunk(1, offset, 1 + 2 * k))
            return 0

        lax.fori_loop(0, 2, both, 0)
        return 0

    lax.fori_loop(0, 4, sides, 0)

    def far(i, _):
        offset = offset_of(i)
        for half in (0, 1):
            for kind in (2, 3):
                gather_copy(half, i, kind, e).wait_recv()
        attend(chunk(0, offset, 2), chunk(1, offset, 2))
        return 0

    lax.fori_loop(0, 4, far, 0)

    for h in range(4):
        latent = (acc[h] / total[h][:, 0:1]).astype(jnp.bfloat16)
        head_out[:, h * 128:(h + 1) * 128] = jnp.dot(
            latent, w_uv[h], preferred_element_type=jnp.float32
        ).astype(jnp.bfloat16)
    get_w.wait()

    first = []
    for half in (0, 1):
        def project(t, _):
            lane = pl.multiple_of(t * 256, 256)
            both = []
            for k in (0, 1):
                column = pl.multiple_of(half * 3584 + k * 1792 + t * 256, 256)
                both.append(jnp.dot(
                    head_out[...], out_w[:, pl.ds(column, 256)], preferred_element_type=jnp.float32
                ).reshape(16, 8, 256))
            tile = jnp.concatenate(both, axis=1).astype(jnp.bfloat16)
            if half == 0:
                part[0, :, :, pl.ds(lane, 256)] = tile
            else:
                for p in range(16):
                    part[1, (p % 4) * 4 + p // 4, :, pl.ds(lane, 256)] = tile[p]
            return 0

        lax.fori_loop(0, 7, project, 0)
        for d in (1, 2, 3):
            to, line = (at_y(d), lax.rem(y + d, 4)) if half == 0 else (at_z(d), lax.rem(z + d, 4))
            copy = pltpu.make_async_remote_copy(
                src_ref=part.at[half, pl.ds(line * 4, 4)], dst_ref=part_in.at[half, d - 1],
                send_sem=r_send.at[half, 0, d - 1], recv_sem=r_recv.at[half, 0, d - 1],
                device_id=to, device_id_type=MESH,
            )
            copy.start()
            first.append(copy)
    second = []
    for half in (0, 1):
        for d in (1, 2, 3):
            first[half * 3 + d - 1].wait_recv()
        own = y if half == 0 else z

        def add(k, _):
            value = part[half, own * 4 + k].astype(jnp.float32)
            for d in range(3):
                value = value + part_in[half, d, k].astype(jnp.float32)
            summed[half, k] = value.astype(jnp.bfloat16)
            return 0

        lax.fori_loop(0, 4, add, 0)
        for d in (1, 2, 3):
            to, line = (at_z(d), lax.rem(z + d, 4)) if half == 0 else (at_y(d), lax.rem(y + d, 4))
            copy = pltpu.make_async_remote_copy(
                src_ref=summed.at[half, line], dst_ref=summed_in.at[half, d - 1],
                send_sem=r_send.at[half, 1, d - 1], recv_sem=r_recv.at[half, 1, d - 1],
                device_id=to, device_id_type=MESH,
            )
            copy.start()
            second.append(copy)
    squares = jnp.zeros((8, 1), jnp.float32)
    for half in (0, 1):
        for d in (1, 2, 3):
            second[half * 3 + d - 1].wait_recv()
        value = summed[half, z if half == 0 else y].astype(jnp.float32)
        for d in range(3):
            value = value + summed_in[half, d].astype(jnp.float32)
        for k in (0, 1):
            q = 2 * half + k
            row = residual[:, q * 1792:(q + 1) * 1792].astype(jnp.float32) + value[k * 8:(k + 1) * 8]
            rows[q] = row
            mixed[:, q * 1792:(q + 1) * 1792] = row
            squares = squares + jnp.sum(row * row, axis=1, keepdims=True)
    norm = lax.rsqrt(squares / 7168.0 + 1e-06)
    for q in (0, 2):
        pair = jnp.concatenate([rows[q] * norm, rows[q + 1] * norm], axis=0)
        normed[q * 8:(q + 2) * 8] = pair.astype(jnp.bfloat16)

    for copy in sent + first + second:
        copy.wait_send()
    for half in (0, 1):
        for group in range(5):
            for kind in range(4):
                gather_copy(half, group if group < 4 else None, kind, e).wait_send()


def attend_call(served, queries, chosen, w_uv, w_out, residual, w_down):
    vmem = pl.BlockSpec(memory_space=pltpu.VMEM)
    anywhere = pl.BlockSpec(memory_space=pl.ANY)
    bf16, f32 = jnp.bfloat16, jnp.float32
    dma = pltpu.SemaphoreType.DMA
    return pl.pallas_call(
        attend_kernel,
        name="attend",
        out_shape=(
            jax.ShapeDtypeStruct((8, 7168), f32),
            jax.ShapeDtypeStruct((32, 1792), bf16),
            jax.ShapeDtypeStruct((2048, 896), bf16),
        ),
        in_specs=[vmem, vmem, vmem, vmem, anywhere, vmem, anywhere],
        out_specs=(vmem, vmem, anywhere),
        scratch_shapes=[
            pltpu.VMEM((16, 256, 576), bf16),
            pltpu.VMEM((4, 128, 576), bf16),
            pltpu.VMEM((4, 128, 256), f32),
            pltpu.VMEM((4, 128, 128), f32),
            pltpu.VMEM((4, 128, 128), f32),
            pltpu.VMEM((4, 128, 512), f32),
            pltpu.VMEM((128, 512), bf16),
            pltpu.VMEM((512, 7168), bf16),
            pltpu.VMEM((2, 16, 16, 1792), bf16),
            pltpu.VMEM((2, 3, 4, 16, 1792), bf16),
            pltpu.VMEM((2, 4, 16, 1792), bf16),
            pltpu.VMEM((2, 3, 16, 1792), bf16),
            pltpu.VMEM((4, 8, 1792), f32),
            dma((7,)), dma((7,)),
            dma((2, 5, 4)), dma((2, 5, 4)),
            dma((2, 2, 3)), dma((2, 2, 3)),
            dma((7,)), dma((7,)),
            dma((2,)),
        ],
        compiler_params=pltpu.CompilerParams(
            collective_id=0, has_side_effects=True, vmem_limit_bytes=56 << 20
        ),
    )(served, queries, chosen, w_uv, w_out, residual, w_down)


def serve(latent_store, group_passages, passage_place):
    s, e = lax.axis_index("store"), lax.axis_index("ep")
    lists = group_passages.reshape(8, 8, 4)
    ids = lax.dynamic_slice(lists, (0, s, e // 4), (8, 1, 1)).reshape(8)
    places = passage_place[ids] - s * 32
    return jax.vmap(
        lambda row: lax.dynamic_slice(latent_store, (row, (e % 4) * 32, 0), (1, 32, 576))[0]
    )(places)


def front(queries, residual_in, latent_store, group_passages, row_slots, passage_place, w_uv, w_out, w_down):
    served = serve(latent_store, group_passages, passage_place)
    chosen = jnp.any(row_slots[:, :, None] == jnp.arange(32, dtype=jnp.int32), axis=1).astype(jnp.bfloat16)
    return attend_call(served, queries, chosen, w_uv, w_out, residual_in, w_down[0])


def build_slots(chosen_ids, expert_count, capacity):
    expert_range = jnp.arange(expert_count, dtype=jnp.int32)
    routed = jnp.sum((chosen_ids[..., None] == expert_range).astype(jnp.int32), axis=-2)
    earlier = jnp.cumsum(routed, axis=-2) - routed
    depth_range = jnp.arange(capacity, dtype=jnp.int32)
    slot_mask = (routed[..., None] == 1) & (earlier[..., None] == depth_range)
    return jnp.moveaxis(slot_mask, -3, -1)


def body(
    queries, residual_in, latent_store, group_passages, row_slots, passage_place, w_uv, w_out,
    expert_ids, expert_gates, w_gate, w_up, w_down,
):
    mixed_rows, normed, _ = front(
        queries, residual_in, latent_store, group_passages, row_slots, passage_place, w_uv, w_out, w_down
    )
    normed = normed.reshape(4, 8, 1792).transpose(1, 0, 2).reshape(8, 7168)
    expert_count, tok_rows, model_width, top_count = 16, 8, 7168, 4
    capacity = min(tok_rows, 2 * ((tok_rows * top_count + expert_count - 1) // expert_count))
    slot_table = build_slots(expert_ids, expert_count, capacity).astype(jnp.bfloat16)
    outgoing = jnp.einsum(
        "ecr,rd->ecd", slot_table, normed, preferred_element_type=jnp.float32
    ).astype(jnp.bfloat16)
    arrived = lax.all_to_all(outgoing, "ep", split_axis=0, concat_axis=0, tiled=True)
    gathered = lax.all_gather(
        arrived.reshape(expert_count * capacity, model_width), "store", axis=0, tiled=True
    )
    row_block = gathered
    gate_proj = jnp.dot(row_block, w_gate[0], preferred_element_type=jnp.float32)
    up_proj = jnp.dot(row_block, w_up[0], preferred_element_type=jnp.float32)
    hidden = (jax.nn.silu(gate_proj) * up_proj).astype(jnp.bfloat16)
    summed = lax.psum_scatter(
        jnp.dot(hidden, w_down[0], preferred_element_type=jnp.float32).astype(jnp.bfloat16),
        "store",
        scatter_dimension=0,
        tiled=True,
    )
    expert_rows = summed.reshape(expert_count, capacity, model_width)
    returned = lax.all_to_all(expert_rows, "ep", split_axis=0, concat_axis=0, tiled=True)
    expert_range = jnp.arange(expert_count, dtype=jnp.int32)
    gate_of = jnp.sum(
        jnp.where(expert_ids[:, :, None] == expert_range, expert_gates[:, :, None], 0.0), axis=1
    )
    weighted = slot_table.astype(jnp.float32) * jnp.transpose(gate_of)[:, None, :]
    expert_mix = jnp.einsum(
        "ecr,ecd->rd", weighted, returned.astype(jnp.float32), precision=lax.Precision.HIGHEST
    )
    return (mixed_rows + expert_mix).astype(jnp.bfloat16)


def solution(mesh):
    return jax.shard_map(
        body,
        mesh=mesh,
        in_specs=(
            P("store", "ep"),
            P(("store", "ep"), None),
            P("store", None, None),
            P(),
            P("store", None),
            P(),
            P("ep", None, None),
            P("ep", None),
            P(("store", "ep"), None),
            P(("store", "ep"), None),
            P("ep", None, "store"),
            P("ep", None, "store"),
            P("ep", "store", None),
        ),
        out_specs=P(("store", "ep"), None),
        check_vma=False,
    )
```

time: 398 us -> 268 us (0.67)
  waiting for transfers between devices: 249 us -> 106 us
  Pallas kernels: 0 us -> 78.8 us
  matrix products: 54.2 us -> 25.2 us
  local copies, waits for them, and re-layouts: 45.7 us -> 18.2 us
  starting transfers between devices: 13 us -> 6.92 us
    unnamed x4 -> x2, waiting for transfers between devices: 87.7 us -> 0.03 us
    pallas_call x0 -> x1, Pallas kernels: none -> 78.8 us  [attend_call(): pl.pallas_call(attend_kernel, name='attend', out_shape=(jax.ShapeDtypeStr...]
    all_to_all x1 -> x0, waiting for transfers between devices: 54.2 us -> none  [body(): lax.all_to_all(served, 'store', split_axis=0, concat_axis=0, tiled=True)]
    reshape x3 -> x1, local copies, waits for them, and re-layouts: 18.5 us -> 0.1 us  [serve(): lists = group_passages.reshape(8, 8, 4)]
    sub x1 -> x0, matrix products: 15.4 us -> none  [body(): exponent = jnp.where(kept_mask, jnp.exp(scores - row_max), 0.0)]
    dot_general x2 -> x0, matrix products: 12.7 us -> none  [the longest x1 7.11 us: body(): jnp.einsum('rhc,hcv->rhv', latent_out, w_uv, preferred_element_type=jnp.f...]
    gather x3, local copies, waits for them, and re-layouts: 15.2 us -> 3.65 us  [the longest x2 3.01 us: serve(): lax.dynamic_slice(latent_store, (row, e % 4 * 32, 0), (1, 32, 576))[0]]
    unnamed x18 -> x13, local copies, waits for them, and re-layouts: 0.92 us -> 9 us
  transfers between devices with their start and end apart: 5 -> 3, of which waited for: 5 -> 3; matrix products, arithmetic and copies ran while one was open for 0% -> 0% of each run, Pallas kernels for 0% -> 0%
where the time goes in v1:
time: 268 us; the launch traced here: 266 us
  waiting for transfers between devices  106 us (40%)
  Pallas kernels  78.8 us (29%)
  matrix products  25.2 us (9%)
  local copies, waits for them, and re-layouts  18.2 us (7%)
  blocking collectives  16.1 us (6%)
  between operations  13.5 us (5%)
  starting transfers between devices  6.92 us (3%)
    pallas_call x1, Pallas kernels, attend_call(): pl.pallas_call(attend_kernel, name='attend', out_shape=(jax.ShapeDtypeStr...  78.8 us
    reduce_scatter x1, waiting for transfers between devices, body(): lax.psum_scatter(jnp.dot(hidden, w_down[0], preferred_element_type=jnp.fl...  46.7 us
    all_gather x1, waiting for transfers between devices, body(): lax.all_gather(arrived.reshape(expert_count * capacity, model_width), 'st...  45.6 us
    all_to_all x1, blocking collectives, body(): lax.all_to_all(outgoing, 'ep', split_axis=0, concat_axis=0, tiled=True)  16.1 us
    dot_general x1, matrix products, body(): jnp.dot(hidden, w_down[0], preferred_element_type=jnp.float32)  16 us
    all_to_all x1, waiting for transfers between devices, body(): lax.all_to_all(expert_rows, 'ep', split_axis=0, concat_axis=0, tiled=True)  13.8 us
    unnamed x13, local copies, waits for them, and re-layouts  9 us
    all_to_all x1, starting transfers between devices, body(): lax.all_to_all(expert_rows, 'ep', split_axis=0, concat_axis=0, tiled=True)  6.7 us
  transfers between devices with their start and end apart: 3, of which 3 were waited for; matrix products, arithmetic and copies ran while one was open for 0% of the time, Pallas kernels for 0%

profile of v1, /device:TPU:1, one launch (start us, length us, event | category | flops | bytes accessed | tf_op | source)
XLA Modules:
  0.0 265.8 jit_solution(6017522336589299216)
XLA Ops:
  6.5 0.8 convert_reduce_fusion
  7.4 9.0 %copy.46 = bf16[32,128,576]{2,0,1:T(8,128)(2,1)} copy(bf16[32,128,576]{1,2,0:T(8,128)(2,1)} %param.15) | data formatting | bytes 9437184 | tf_op args[2]
  16.3 0.1 reshape.81
  16.5 0.3 dynamic-slice_reduce_fusion
  16.8 0.6 gather_fusion
  17.5 2.3 gather_fusion.1
  19.7 0.8 copy.47.served
  20.5 0.7 copy.48.chosen
  21.3 78.8 %attend.1 = (f32[8,7168]{1,0:T(8,128)}, bf16[32,1792]{1,0:T(8,128)(2,1)}, bf16[2048,896]{1,0:T(8,128)(2,1)}) custom-call(bf16[8,32,576]{2,1,0:T(8,128)(2,1)} %copy.47.served, bf16[128,2304]{1,0:T(8,128)(2,1)} %queries.1, bf16[128,32]{1,0:T(8,128)(2,1)} %copy.48.chosen, bf16[4,512,128]{2,1,0:T(8,128)(2,1)} %w_uv.1, bf16[512,7168]{1,0:T(8,128)(2,1)} %w_out.1, ...), custom_call_target="tpu_custom_call" | custom-call | tf_op jit(solution)/shard_map/attend/pallas_call | solution.py:250
  100.1 1.3 convolution_convert_fusion.1
  101.4 0.7 copy.49
  102.1 16.1 %all_to_all.10 = bf16[16,4,7168]{2,1,0:T(4,128)(2,1)S(1)} all-to-all(bf16[16,4,7168]{2,1,0:T(4,128)(2,1)S(1)} %copy.49), channel_id=1, replica_groups=mesh['store'=8,'ep'=16] {'ep'}, dimensions={0} | all-to-all | bytes 1835008 | tf_op jit(solution)/shard_map/all_to_all | solution.py:325
  118.2 1.1 reshape.85
  119.3 0.0 all-gather.2.cloned.1.call-update
  119.3 0.2 reduce-scatter.2.cloned.1.call-start
  119.6 45.6 %all-gather.2.cloned.1.call-done = bf16[512,7168]{1,0:T(8,128)(2,1)} async-done(((bf16[64,7168]{1,0:T(8,128)(2,1)}), bf16[512,7168]{1,0:T(8,128)(2,1)}) %all-gather.2.cloned.1.call-update) | async-done | bytes 7340048 | tf_op jit(solution)/shard_map/all_gather | solution.py:326
  165.1 6.2 %fusion.4 = f32[512,256]{1,0:T(8,128)S(1)} fusion(bf16[512,7168]{1,0:T(8,128)(2,1)} %all-gather.2.cloned.1.call-done, bf16[1,7168,256]{2,1,0:T(8,128)(2,1)} %param.23), kind=kOutput, calls=%fused_computation.9 | convolution fusion | flops 1879048192 | bytes 11534336 | tf_op jit(solution)/shard_map/dot_general | solution.py:330
  171.3 16.0 %convolution_convert_fusion = bf16[512,7168]{1,0:T(8,128)(2,1)} fusion(bf16[1,256,7168]{2,1,0:T(8,128)(2,1)} %param.25, bf16[512,7168]{1,0:T(8,128)(2,1)} %all-gather.2.cloned.1.call-done, bf16[1,7168,256]{2,1,0:T(8,128)(2,1)} %param.24, f32[512,256]{1,0:T(8,128)S(1)} %fusion.4), kind=kOutput, calls=%fused_computation.2 | convolution fusion | flops 3762552832 | bytes 22544384 | tf_op jit(solution)/shard_map/dot_general | solution.py:334
  187.4 46.7 %reduce-scatter.2.cloned.1.call-done = bf16[64,7168]{1,0:T(8,128)(2,1)} async-done(((bf16[512,7168]{1,0:T(8,128)(2,1)}), bf16[64,7168]{1,0:T(8,128)(2,1)}) %reduce-scatter.2.cloned.1.call-update) | async-done | bytes 917520 | tf_op jit(solution)/shard_map/reduce_scatter | solution.py:333
  234.1 2.5 reshape.86
  236.6 6.7 %all-to-all-start.1 = ((bf16[16,4,7168]{2,1,0:T(4,128)(2,1)}), bf16[16,4,7168]{2,1,0:T(4,128)(2,1)S(1)}, u32[]{:S(2)}, u32[]{:S(2)}) async-start(bf16[16,4,7168]{2,1,0:T(4,128)(2,1)} %reshape.86), calls=%async_computation.2 | async-start | bytes 1835008 | tf_op jit(solution)/shard_map/all_to_all | solution.py:340
  243.4 0.1 select_reduce_fusion
  243.4 13.8 %all-to-all-done.1 = bf16[16,4,7168]{2,1,0:T(4,128)(2,1)S(1)} async-done(((bf16[16,4,7168]{2,1,0:T(4,128)(2,1)}), bf16[16,4,7168]{2,1,0:T(4,128)(2,1)S(1)}, u32[]{:S(2)}, u32[]{:S(2)}) %all-to-all-start.1) | async-done | bytes 917536 | tf_op jit(solution)/shard_map/all_to_all | solution.py:340
  257.2 1.7 fusion.1
  (22 shorter events, 0.1 us)
Async XLA Ops:
  6.5 10.3 %copy-start = (s32[256]{0:T(256)S(1)}, s32[256]{0:T(256)}, u32[]{:S(2)}) copy-start(s32[256]{0:T(256)} %param.18) | copy-start | bytes 3076
  6.5 158.6 %all-gather.2.cloned.1.call-start = ((), (), s32[]{:S(2)}) async-start(), calls=%async_computation.3 | async-start | bytes 8257536 | tf_op jit(solution)/shard_map/all_gather | solution.py:326
  7.3 9.0 %copy-start.5 = (s32[256]{0:T(256)S(1)}, s32[256]{0:T(256)}, u32[]{:S(2)}) copy-start(s32[256]{0:T(256)} %param.16) | copy-start | bytes 3076
  7.3 13.1 %copy-start.2 = (s32[128,16]{0,1:T(8,128)S(1)}, s32[128,16]{0,1:T(8,128)}, u32[]{:S(2)}) copy-start(s32[128,16]{0,1:T(8,128)} %param.17) | copy-start | bytes 24580
  119.3 114.8 %reduce-scatter.2.cloned.1.call-start = ((), (), s32[]{:S(2)}) async-start(), calls=%async_computation.4 | async-start | bytes 8257536 | tf_op jit(solution)/shard_map/reduce_scatter | solution.py:333
  187.3 56.0 %copy-start.3 = (s32[8,4]{0,1:T(4,128)S(1)}, s32[8,4]{0,1:T(4,128)}, u32[]{:S(2)}) copy-start(s32[8,4]{0,1:T(4,128)} %param.21) | copy-start | bytes 388
  187.3 56.0 %copy-start.4 = (f32[8,4]{0,1:T(4,128)S(1)}, f32[8,4]{0,1:T(4,128)}, u32[]{:S(2)}) copy-start(f32[8,4]{0,1:T(4,128)} %param.22) | copy-start | bytes 388
  187.3 69.9 %copy-start.1 = (f32[8,7168]{1,0:T(8,128)S(1)}, f32[8,7168]{1,0:T(8,128)}, u32[]{:S(2)}) copy-start(f32[8,7168]{1,0:T(8,128)} %get-tuple-element.7) | copy-start | bytes 688132
  236.6 20.6 %all-to-all-start.1 = ((bf16[16,4,7168]{2,1,0:T(4,128)(2,1)}), bf16[16,4,7168]{2,1,0:T(4,128)(2,1)S(1)}, u32[]{:S(2)}, u32[]{:S(2)}) async-start(bf16[16,4,7168]{2,1,0:T(4,128)(2,1)} %reshape.86), calls=%async_computation.2 | async-start | bytes 1835008 | tf_op jit(solution)/shard_map/all_to_all | solution.py:340
Sparse Core Ops, SparseCore 0:
  119.5 45.6 all-gather.1
  187.5 46.5 reduce-scatter.1

commit v2 on v1

--- a/solution.py
+++ b/solution.py
@@ -111,6 +111,22 @@
         copy.wait_recv()
     launch(None, 0)
     launch(0, 0)
+    keep_w = pltpu.make_async_copy(
+        w_down.at[:, pl.ds(pl.multiple_of(s * 896, 896), 896)],
+        down_cols.at[pl.ds(pl.multiple_of(s * 256, 256), 256)], w_sem.at[1],
+    )
+    keep_w.start()
+    moved = []
+    for d in range(1, 8):
+        to = at_s(d)
+        copy = pltpu.make_async_remote_copy(
+            src_ref=w_down.at[:, pl.ds(pl.multiple_of(to[0] * 896, 896), 896)],
+            dst_ref=down_cols.at[pl.ds(pl.multiple_of(s * 256, 256), 256)],
+            send_sem=d_send.at[d - 1], recv_sem=d_recv.at[d - 1],
+            device_id=to, device_id_type=MESH,
+        )
+        copy.start()
+        moved.append(copy)
     attend(e, e)
     for kind in (0, 1):
         offset = 1 if kind == 0 else 3
@@ -234,7 +250,10 @@
         pair = jnp.concatenate([rows[q] * norm, rows[q + 1] * norm], axis=0)
         normed[q * 8:(q + 2) * 8] = pair.astype(jnp.bfloat16)
 
-    for copy in sent + first + second:
+    keep_w.wait()
+    for copy in moved:
+        copy.wait_recv()
+    for copy in sent + first + second + moved:
         copy.wait_send()
     for half in (0, 1):
         for group in range(5):
@@ -299,54 +318,288 @@
     return attend_call(served, queries, chosen, w_uv, w_out, residual_in, w_down[0])
 
 
-def build_slots(chosen_ids, expert_count, capacity):
-    expert_range = jnp.arange(expert_count, dtype=jnp.int32)
-    routed = jnp.sum((chosen_ids[..., None] == expert_range).astype(jnp.int32), axis=-2)
-    earlier = jnp.cumsum(routed, axis=-2) - routed
-    depth_range = jnp.arange(capacity, dtype=jnp.int32)
-    slot_mask = (routed[..., None] == 1) & (earlier[..., None] == depth_range)
-    return jnp.moveaxis(slot_mask, -3, -1)
+def expert_kernel(
+    normed, mixed, place, weigh, w_gate, w_up, down_cols,
+    out,
+    outgoing, arrived, x_rows, w_in, w_down, pre, hid, y_part, y_rows, back, returned,
+    t_send, t_recv, a_send, a_recv, h_send, h_recv, y_send, y_recv, b_send, b_recv, w_sem,
+):
+    s = lax.axis_index("store")
+    e = lax.axis_index("ep")
+    y, z = e // 4, e % 4
+    sibling = s + 1 - 2 * (s % 2)
+
+    def on_store(d):
+        return lax.rem(s + d, 8)
+
+    def on_ep(dy, dz):
+        return lax.rem(y + dy, 4) * 4 + lax.rem(z + dz, 4)
+
+    barrier = pltpu.get_barrier_semaphore()
+    peers = [(on_store(d), e) for d in range(1, 8)]
+    peers += [(s, on_ep(dy, dz)) for dy in range(4) for dz in range(4) if dy or dz]
+    for peer in peers:
+        pl.semaphore_signal(barrier, inc=1, device_id=peer, device_id_type=MESH)
+    loads = [
+        pltpu.make_async_copy(w_gate, w_in.at[:, 0:256], w_sem.at[0]),
+        pltpu.make_async_copy(w_up, w_in.at[:, 256:512], w_sem.at[1]),
+        pltpu.make_async_copy(down_cols, w_down, w_sem.at[2]),
+    ]
+    for load in loads:
+        load.start()
+    outgoing[...] = jnp.dot(
+        place[...], normed[...], preferred_element_type=jnp.float32
+    ).astype(jnp.bfloat16).reshape(16, 16, 1792)
+    pl.semaphore_wait(barrier, len(peers))
+
+    def copy_to(src, dst, send, recv, device):
+        return pltpu.make_async_remote_copy(
+            src_ref=src, dst_ref=dst, send_sem=send, recv_sem=recv, device_id=device, device_id_type=MESH
+        )
+
+    def dispatch(k, dz):
+        to = on_ep(offset_of(k), dz)
+        return copy_to(outgoing.at[to], arrived.at[e], t_send.at[k, dz], t_recv.at[k, dz], (s, to))
+
+    def give_back(k, dz):
+        to = on_ep(4 - offset_of(k), dz)
+        return copy_to(back.at[k, lax.rem(z + dz, 4)], returned.at[e], b_send.at[k, dz], b_recv.at[k, dz], (s, to))
+
+    def gather(k, kind):
+        to = {0: 2, 1: 6, 2: 2, 3: 6}.get(kind)
+        to = sibling if to is None else on_store(to)
+        block = on_store((0, 0, 6, 2, 0, 6, 2, 4, 4)[kind])
+        low = pl.multiple_of(block * 16, 16)
+        columns = {2: (0, 3584), 3: (3584, 3584), 7: (0, 3584), 8: (3584, 3584)}.get(kind, (0, 7168))
+        ref = x_rows.at[k, pl.ds(low, 16), pl.ds(*columns)]
+        return copy_to(ref, ref, a_send.at[k, kind], a_recv.at[k, kind], (to, e))
+
+    def share(k, kind):
+        to = on_store((2, 6, 4)[kind]) if kind < 3 else sibling
+        block = on_store((0, 0, 0, 0, 6, 2, 4)[kind])
+        ref = hid.at[k, :, pl.ds(pl.multiple_of(block * 256, 256), 256)]
+        return copy_to(ref, ref, h_send.at[k, kind], h_recv.at[k, kind], (to, e))
+
+    def hand_over(k, d):
+        to = on_store(d)
+        return copy_to(
+            y_part.at[k, pl.ds(pl.multiple_of(to * 16, 16), 16)],
+            y_rows.at[k, :, pl.ds(pl.multiple_of(s * 896, 896), 896)],
+            y_send.at[k, d - 1], y_recv.at[k, d - 1], (to, e),
+        )
+
+    for k in range(4):
+        for dz in (0, 1, 3, 2):
+            if k or dz:
+                dispatch(k, dz).start()
+    arrived[e] = outgoing[e]
+
+    rows16 = lax.broadcasted_iota(jnp.int32, (16, 64), 0)
+    cols64 = lax.broadcasted_iota(jnp.int32, (16, 64), 1)
+    rows64 = lax.broadcasted_iota(jnp.int32, (64, 16), 0)
+    cols16 = lax.broadcasted_iota(jnp.int32, (64, 16), 1)
+
+    def take(q):
+        return (cols64 == (rows16 // 4) * 16 + q * 4 + rows16 % 4).astype(jnp.bfloat16)
+
+    def put(q):
+        return (rows64 == (cols16 // 4) * 16 + q * 4 + cols16 % 4).astype(jnp.bfloat16)
+
+    def enter(k):
+        for dz in range(1, 4):
+            dispatch(k, dz).wait_recv()
+
+        @pl.when(k > 0)
+        def _():
+            dispatch(k, 0).wait_recv()
+
+        line = lax.rem(y + 4 - offset_of(k), 4)
+        block = arrived[pl.ds(line * 4, 4)].reshape(64, 1792)
+        for q in range(4):
+            x_rows[k, pl.ds(pl.multiple_of(s * 16, 16), 16), q * 1792:(q + 1) * 1792] = jnp.dot(
+                take(q), block, preferred_element_type=jnp.float32
+            ).astype(jnp.bfloat16)
+        for kind in (0, 1, 4):
+            gather(k, kind).start()
+
+    def pass_on(k):
+        for kind in (0, 1):
+            gather(k, kind).wait_recv()
+            gather(k, kind + 2).start()
+            gather(k, kind + 5).start()
+
+    def hidden(k):
+        for kind in (2, 3):
+            gather(k, kind).wait_recv()
+            gather(k, kind + 5).start()
+        for kind in range(4, 9):
+            gather(k, kind).wait_recv()
+        pre[...] = jnp.zeros_like(pre)
+
+        def add(q, _):
+            low = pl.multiple_of(q * 1792, 1792)
+            pre[...] += jnp.dot(
+                x_rows[k, :, pl.ds(low, 1792)], w_in[pl.ds(low, 1792)], preferred_element_type=jnp.float32
+            )
+            return 0
+
+        lax.fori_loop(0, 4, add, 0)
+        gate = pre[:, 0:256]
+        hid[k, :, pl.ds(pl.multiple_of(s * 256, 256), 256)] = (
+            gate / (1.0 + jnp.exp(-gate)) * pre[:, 256:512]
+        ).astype(jnp.bfloat16)
+        for kind in range(4):
+            share(k, kind).start()
+
+    def project(k):
+        for kind in range(3):
+            share(k, kind).wait_recv()
+            share(k, kind + 4).start()
+        for kind in range(3, 7):
+            share(k, kind).wait_recv()
+        y_part[k] = jnp.dot(hid[k], w_down[...], preferred_element_type=jnp.float32).astype(jnp.bfloat16)
+        for d in range(1, 8):
+            hand_over(k, d).start()
+        y_rows[k, :, pl.ds(pl.multiple_of(s * 896, 896), 896)] = y_part[k, pl.ds(pl.multiple_of(s * 16, 16), 16)]
+
+    def leave(k):
+        for d in range(1, 8):
+            hand_over(k, d).wait_recv()
+        total = jnp.zeros((64, 1792), jnp.float32)
+        for q in range(4):
+            total = total + jnp.dot(
+                put(q), y_rows[k, :, q * 1792:(q + 1) * 1792], preferred_element_type=jnp.float32
+            )
+        back[k] = total.astype(jnp.bfloat16).reshape(4, 16, 1792)
+        for dz in range(1, 4):
+            give_back(k, dz).start()
+
+        @pl.when(k > 0)
+        def _():
+            give_back(k, 0).start()
+
+        @pl.when(k == 0)
+        def _():
+            returned[e] = back[k, z]
+
+    def step(t, _):
+        @pl.when(t < 4)
+        def _():
+            enter(t)
+
+        @pl.when(t == 1)
+        def _():
+            for load in loads:
+                load.wait()
+
+        @pl.when((t >= 1) & (t < 5))
+        def _():
+            hidden(t - 1)
+
+        @pl.when(t < 4)
+        def _():
+            pass_on(t)
+
+        @pl.when((t >= 2) & (t < 6))
+        def _():
+            project(t - 2)
+
+        @pl.when(t >= 3)
+        def _():
+            leave(t - 3)
+
+        return 0
+
+    lax.fori_loop(0, 7, step, 0)
+
+    for k in range(4):
+        for dz in range(4):
+            if k or dz:
+                give_back(k, dz).wait_recv()
+    rows = returned[...].reshape(256, 1792)
+    total = jnp.dot(weigh[0], rows, preferred_element_type=jnp.float32) + jnp.dot(
+        weigh[1], rows, preferred_element_type=jnp.float32
+    )
+    for q in range(4):
+        out[:, q * 1792:(q + 1) * 1792] = (
+            mixed[:, q * 1792:(q + 1) * 1792] + total[q * 8:(q + 1) * 8]
+        ).astype(jnp.bfloat16)
+
+    for k in range(4):
+        for dz in range(4):
+            if k or dz:
+                dispatch(k, dz).wait_send()
+                give_back(k, dz).wait_send()
+        for kind in range(9):
+            gather(k, kind).wait_send()
+        for kind in range(7):
+            share(k, kind).wait_send()
+            hand_over(k, kind + 1).wait_send()
+
+
+def expert_call(normed, mixed, place, weigh, w_gate, w_up, down_cols):
+    vmem = pl.BlockSpec(memory_space=pltpu.VMEM)
+    anywhere = pl.BlockSpec(memory_space=pl.ANY)
+    bf16, f32 = jnp.bfloat16, jnp.float32
+    dma = pltpu.SemaphoreType.DMA
+    return pl.pallas_call(
+        expert_kernel,
+        name="experts",
+        out_shape=jax.ShapeDtypeStruct((8, 7168), bf16),
+        in_specs=[vmem, vmem, vmem, vmem, anywhere, anywhere, anywhere],
+        out_specs=vmem,
+        scratch_shapes=[
+            pltpu.VMEM((16, 16, 1792), bf16),
+            pltpu.VMEM((16, 16, 1792), bf16),
+            pltpu.VMEM((4, 128, 7168), bf16),
+            pltpu.VMEM((7168, 512), bf16),
+            pltpu.VMEM((2048, 896), bf16),
+            pltpu.VMEM((128, 512), f32),
+            pltpu.VMEM((4, 128, 2048), bf16),
+            pltpu.VMEM((4, 128, 896), bf16),
+            pltpu.VMEM((4, 16, 7168), bf16),
+            pltpu.VMEM((4, 4, 16, 1792), bf16),
+            pltpu.VMEM((16, 16, 1792), bf16),
+            dma((4, 4)), dma((4, 4)),
+            dma((4, 9)), dma((4, 9)),
+            dma((4, 7)), dma((4, 7)),
+            dma((4, 7)), dma((4, 7)),
+            dma((4, 4)), dma((4, 4)),
+            dma((3,)),
+        ],
+        compiler_params=pltpu.CompilerParams(
+            collective_id=1, has_side_effects=True, vmem_limit_bytes=56 << 20
+        ),
+    )(normed, mixed, place, weigh, w_gate, w_up, down_cols)
+
+
+def routing(expert_ids, expert_gates):
+    experts = jnp.arange(16, dtype=jnp.int32)
+    named = (expert_ids[:, :, None] == experts).astype(jnp.float32)
+    routed = jnp.sum(named, axis=1)
+    gate = jnp.sum(named * expert_gates[:, :, None], axis=1)
+    earlier = jnp.cumsum(routed, axis=0) - routed
+    depth = jnp.arange(4, dtype=jnp.float32)
+    slot = jnp.where((routed[..., None] > 0.5) & (earlier[..., None] == depth), 1.0, 0.0)
+    eye = jnp.eye(4, dtype=jnp.float32)
+    place = jnp.einsum("rec,qp->eqcpr", slot, eye).reshape(256, 32).astype(jnp.bfloat16)
+    held = slot * gate[..., None]
+    high = held.astype(jnp.bfloat16)
+    low = (held - high.astype(jnp.float32)).astype(jnp.bfloat16)
+    weigh = jnp.stack([high, low]).astype(jnp.float32)
+    weigh = jnp.einsum("nrec,qp->nqrepc", weigh, eye).reshape(2, 32, 256).astype(jnp.bfloat16)
+    return place, weigh
 
 
 def body(
     queries, residual_in, latent_store, group_passages, row_slots, passage_place, w_uv, w_out,
     expert_ids, expert_gates, w_gate, w_up, w_down,
 ):
-    mixed_rows, normed, _ = front(
+    mixed, normed, down_cols = front(
         queries, residual_in, latent_store, group_passages, row_slots, passage_place, w_uv, w_out, w_down
     )
-    normed = normed.reshape(4, 8, 1792).transpose(1, 0, 2).reshape(8, 7168)
-    expert_count, tok_rows, model_width, top_count = 16, 8, 7168, 4
-    capacity = min(tok_rows, 2 * ((tok_rows * top_count + expert_count - 1) // expert_count))
-    slot_table = build_slots(expert_ids, expert_count, capacity).astype(jnp.bfloat16)
-    outgoing = jnp.einsum(
-        "ecr,rd->ecd", slot_table, normed, preferred_element_type=jnp.float32
-    ).astype(jnp.bfloat16)
-    arrived = lax.all_to_all(outgoing, "ep", split_axis=0, concat_axis=0, tiled=True)
-    gathered = lax.all_gather(
-        arrived.reshape(expert_count * capacity, model_width), "store", axis=0, tiled=True
-    )
-    row_block = gathered
-    gate_proj = jnp.dot(row_block, w_gate[0], preferred_element_type=jnp.float32)
-    up_proj = jnp.dot(row_block, w_up[0], preferred_element_type=jnp.float32)
-    hidden = (jax.nn.silu(gate_proj) * up_proj).astype(jnp.bfloat16)
-    summed = lax.psum_scatter(
-        jnp.dot(hidden, w_down[0], preferred_element_type=jnp.float32).astype(jnp.bfloat16),
-        "store",
-        scatter_dimension=0,
-        tiled=True,
-    )
-    expert_rows = summed.reshape(expert_count, capacity, model_width)
-    returned = lax.all_to_all(expert_rows, "ep", split_axis=0, concat_axis=0, tiled=True)
-    expert_range = jnp.arange(expert_count, dtype=jnp.int32)
-    gate_of = jnp.sum(
-        jnp.where(expert_ids[:, :, None] == expert_range, expert_gates[:, :, None], 0.0), axis=1
-    )
-    weighted = slot_table.astype(jnp.float32) * jnp.transpose(gate_of)[:, None, :]
-    expert_mix = jnp.einsum(
-        "ecr,ecd->rd", weighted, returned.astype(jnp.float32), precision=lax.Precision.HIGHEST
-    )
-    return (mixed_rows + expert_mix).astype(jnp.bfloat16)
+    place, weigh = routing(expert_ids, expert_gates)
+    return expert_call(normed, mixed, place, weigh, w_gate[0], w_up[0], down_cols)
 
 
 def solution(mesh):

time: 268 us -> 188 us (0.70)
  waiting for transfers between devices: 106 us -> 0 us
  Pallas kernels: 78.8 us -> 167 us
  matrix products: 25.2 us -> 0 us
  blocking collectives: 16.1 us -> 0 us
  between operations: 13.5 us -> 0.16 us
  starting transfers between devices: 6.92 us -> 0 us
    pallas_call x0 -> x1, Pallas kernels: none -> 88.2 us  [expert_call(): pl.pallas_call(expert_kernel, name='experts', out_shape=jax.ShapeDtypeStr...]
    reduce_scatter x1 -> x0, waiting for transfers between devices: 46.7 us -> none  [body(): lax.psum_scatter(jnp.dot(hidden, w_down[0], preferred_element_type=jnp.fl...]
    all_gather x1 -> x0, waiting for transfers between devices: 45.6 us -> none  [body(): lax.all_gather(arrived.reshape(expert_count * capacity, model_width), 'st...]
    dot_general x4 -> x0, matrix products: 25.2 us -> none  [the longest x1 16 us: body(): jnp.dot(hidden, w_down[0], preferred_element_type=jnp.float32)]
    all_to_all x1 -> x0, blocking collectives: 16.1 us -> none  [body(): lax.all_to_all(outgoing, 'ep', split_axis=0, concat_axis=0, tiled=True)]
    all_to_all x1 -> x0, waiting for transfers between devices: 13.8 us -> none  [body(): lax.all_to_all(expert_rows, 'ep', split_axis=0, concat_axis=0, tiled=True)]
    all_to_all x1 -> x0, starting transfers between devices: 6.7 us -> none  [body(): lax.all_to_all(expert_rows, 'ep', split_axis=0, concat_axis=0, tiled=True)]
    reshape x2 -> x0, local copies, waits for them, and re-layouts: 3.66 us -> none  [the longest x1 2.53 us: body(): expert_rows = summed.reshape(expert_count, capacity, model_width)]
  transfers between devices with their start and end apart: 3 -> 0, of which waited for: 3 -> 0; matrix products, arithmetic and copies ran while one was open for 0% -> 0% of each run, Pallas kernels for 0% -> 0%
where the time goes in v2:
time: 188 us; the launch traced here: 186 us
  Pallas kernels  167 us (89%)
  local copies, waits for them, and re-layouts  18.1 us (10%)
    pallas_call x1, Pallas kernels, expert_call(): pl.pallas_call(expert_kernel, name='experts', out_shape=jax.ShapeDtypeStr...  88.2 us
    pallas_call x1, Pallas kernels, attend_call(): pl.pallas_call(attend_kernel, name='attend', out_shape=(jax.ShapeDtypeStr...  78.8 us
    unnamed x10, local copies, waits for them, and re-layouts  10.5 us

profile of v2, /device:TPU:1, one launch (start us, length us, event | category | flops | bytes accessed | tf_op | source)
XLA Modules:
  0.0 186.1 jit_solution(13209904847852374491)
XLA Ops:
  0.0 0.0 copy-start
  0.0 0.8 reshape.100
  0.8 0.3 dynamic-slice_reduce_fusion
  1.1 0.6 gather_fusion
  1.8 0.0 copy-start.1
  1.8 9.0 %copy.45 = bf16[32,128,576]{2,0,1:T(8,128)(2,1)} copy(bf16[32,128,576]{1,2,0:T(8,128)(2,1)} %param.15) | data formatting | bytes 9437184 | tf_op args[2]
  10.8 2.2 %gather_fusion.1 = bf16[8,32,576]{2,0,1:T(8,128)(2,1)S(1)} fusion(bf16[32,128,576]{2,0,1:T(8,128)(2,1)} %copy.45, s32[8]{0:T(128)S(1)} %fusion.12), kind=kCustom, calls=%fused_computation.1 | custom fusion | bytes 589920 | tf_op jit(solution)/shard_map/vmap()/gather | solution.py:311
  13.1 0.8 copy.46.served
  13.9 0.7 copy.47.chosen
  14.6 78.8 %attend.1 = (f32[8,7168]{1,0:T(8,128)}, bf16[32,1792]{1,0:T(8,128)(2,1)}, bf16[2048,896]{1,0:T(8,128)(2,1)}) custom-call(bf16[8,32,576]{2,1,0:T(8,128)(2,1)} %copy.46.served, bf16[128,2304]{1,0:T(8,128)(2,1)} %queries.1, bf16[128,32]{1,0:T(8,128)(2,1)} %copy.47.chosen, bf16[4,512,128]{2,1,0:T(8,128)(2,1)} %w_uv.1, bf16[512,7168]{1,0:T(8,128)(2,1)} %w_out.1, ...), custom_call_target="tpu_custom_call" | custom-call | tf_op jit(solution)/shard_map/attend/pallas_call | solution.py:269
  93.4 0.0 copy-done.2
  93.4 0.0 copy-done.3
  93.4 0.1 select_reduce_fusion
  93.6 0.1 copy.50
  93.6 0.1 copy.49
  93.7 0.1 copy.53
  93.9 0.3 fusion
  94.2 0.3 convert_element_type.66
  94.5 0.7 copy.54.weigh
  95.2 0.1 copy.48
  95.3 0.2 fusion.1
  95.5 0.8 convert_element_type.60.place
  96.3 88.2 %experts.1 = bf16[8,7168]{1,0:T(8,128)(2,1)} custom-call(bf16[32,1792]{1,0:T(8,128)(2,1)} %get-tuple-element.8.normed, f32[8,7168]{1,0:T(8,128)} %get-tuple-element.9.mixed, bf16[256,32]{1,0:T(8,128)(2,1)} %convert_element_type.60.place, bf16[2,32,256]{2,1,0:T(8,128)(2,1)} %copy.54.weigh, bf16[7168,256]{1,0:T(8,128)(2,1)} %bitcast.18, ...), custom_call_target="tpu_custom_call" | custom-call | tf_op jit(solution)/shard_map/experts/pallas_call | solution.py:545
  184.5 1.6 copy.56
  (16 shorter events, 0.2 us)
Async XLA Ops:
  0.0 1.1 copy-start
  1.8 12.0 %copy-start.1 = (s32[128,16]{0,1:T(8,128)S(1)}, s32[128,16]{0,1:T(8,128)}, u32[]{:S(2)}) copy-start(s32[128,16]{0,1:T(8,128)} %param.17) | copy-start | bytes 24580
  14.6 78.8 %copy-start.2 = (f32[8,4]{0,1:T(4,128)S(1)}, f32[8,4]{0,1:T(4,128)}, u32[]{:S(2)}) copy-start(f32[8,4]{0,1:T(4,128)} %param.22) | copy-start | bytes 388
  14.6 78.8 %copy-start.3 = (s32[8,4]{0,1:T(4,128)S(1)}, s32[8,4]{0,1:T(4,128)}, u32[]{:S(2)}) copy-start(s32[8,4]{0,1:T(4,128)} %param.21) | copy-start | bytes 388

commit v3 on v2

--- a/solution.py
+++ b/solution.py
@@ -7,9 +7,10 @@
 from jax.experimental.pallas import tpu as pltpu
 from jax.sharding import PartitionSpec as P
 
-score_scale = 192.0 ** (-0.5)
+SCALE = 192.0 ** (-0.5) * 1.4426950408889634
 MESH = pl.DeviceIdType.MESH
-LOW = -1e30
+LOW = -1e29
+FAR_LOW = 1e30
 
 
 def offset_of(i):
@@ -17,7 +18,7 @@
 
 
 def attend_kernel(
-    served, queries, chosen, w_uv, w_out, residual, w_down,
+    served, served_far, queries, row_slots, w_uv, w_out, residual, w_down,
     mixed, normed, down_cols,
     kv, heads, mask, top, total, acc, head_out, out_w, part, part_in, summed, summed_in, rows,
     x_send, x_recv, g_send, g_recv, r_send, r_recv, d_send, d_recv, w_sem,
@@ -35,6 +36,9 @@
     def at_s(d):
         return (lax.rem(s + d, 8), e)
 
+    def quarter(q):
+        return pl.ds(pl.multiple_of(q * 144, 16), 144)
+
     peers = [at_s(d) for d in range(1, 8)] + [at_y(d) for d in (1, 2, 3)] + [at_z(d) for d in (1, 2, 3)]
     barrier = pltpu.get_barrier_semaphore()
     for peer in peers:
@@ -47,54 +51,83 @@
     for d in range(1, 8):
         to = at_s(d)
         copy = pltpu.make_async_remote_copy(
-            src_ref=served.at[to[0]],
-            dst_ref=kv.at[e, pl.ds(pl.multiple_of(s * 32, 32), 32)],
-            send_sem=x_send.at[d - 1], recv_sem=x_recv.at[d - 1],
+            src_ref=served.at[to[0]], dst_ref=kv.at[y, s, quarter(z)],
+            send_sem=x_send.at[0, d - 1], recv_sem=x_recv.at[0, d - 1],
             device_id=to, device_id_type=MESH,
         )
         copy.start()
         sent.append(copy)
-    kv[e, pl.ds(pl.multiple_of(s * 32, 32), 32)] = served[s]
+    keep = pltpu.make_async_copy(served.at[s], kv.at[y, s, quarter(z)], w_sem.at[2])
+    keep.start()
+
+    def far_copies(whole):
+        def target(ref):
+            return ref.at[lax.rem(y + 2, 4), s] if whole else ref.at[:, s, quarter(lax.rem(z + 2, 4))]
+
+        def source(g):
+            return served_far.at[g].reshape(576, 128) if whole else served_far.at[g]
+
+        return [
+            pltpu.make_async_remote_copy(
+                src_ref=source(at_s(d)[0]), dst_ref=target(kv),
+                send_sem=x_send.at[1, d - 1], recv_sem=x_recv.at[1, d - 1],
+                device_id=at_s(d), device_id_type=MESH,
+            )
+            for d in range(1, 8)
+        ] + [pltpu.make_async_copy(source(s), target(kv), w_sem.at[3])]
+
+    def each_far(act):
+        for whole in (False, True):
+            @pl.when((s >= 4) if whole else (s < 4))
+            def _():
+                for copy in far_copies(whole):
+                    act(copy)
 
     for h in range(4):
-        heads[h] = queries[:, h * 576:(h + 1) * 576]
-    slot_row = lax.broadcasted_iota(jnp.int32, (32, 256), 0)
-    token_col = lax.broadcasted_iota(jnp.int32, (32, 256), 1)
+        heads[h * 128:(h + 1) * 128] = queries[:, h * 576:(h + 1) * 576]
+    slot = lax.broadcasted_iota(jnp.int32, (32, 128), 0)
+    chosen = jnp.zeros((32, 128), jnp.bool_)
+    for i in range(16):
+        chosen = chosen | (row_slots[i:i + 1] == slot)
+    chosen = chosen.astype(jnp.bfloat16)
+    slot_row = lax.broadcasted_iota(jnp.int32, (32, 512), 0)
+    token_col = lax.broadcasted_iota(jnp.int32, (32, 512), 1)
     for j in range(4):
-        spread = (slot_row == (token_col // 32) * 4 + j).astype(jnp.bfloat16)
-        mask[j] = jnp.dot(chosen[...], spread, preferred_element_type=jnp.float32)
+        for half in (0, 1):
+            spread = (slot_row == (token_col // 128 + 4 * half) * 4 + j).astype(jnp.bfloat16)
+            live = lax.dot_general(
+                chosen, spread, (((0,), (0,)), ((), ())), preferred_element_type=jnp.float32
+            )
+            mask[j, half] = (live - 1.0) * FAR_LOW
     top[...] = jnp.full_like(top, LOW)
     total[...] = jnp.zeros_like(total)
     acc[...] = jnp.zeros_like(acc)
 
     def chunk(half, first, second):
         dy, dz = (first, second) if half == 0 else (second, first)
-        return lax.rem(y - dy + 4, 4) * 4 + lax.rem(z - dz + 4, 4)
-
-    def attend(p_a, p_b):
-        keys = jnp.concatenate([kv[p_a, 0:128], kv[p_b, 128:256]], axis=0)
-        live = jnp.concatenate([mask[p_a // 4][:, 0:128], mask[p_b // 4][:, 128:256]], axis=1)
-        for h in range(4):
-            scores = lax.dot_general(
-                heads[h], keys, (((1,), (1,)), ((), ())), preferred_element_type=jnp.float32
-            ) * score_scale
-            scores = jnp.where(live > 0.5, scores, LOW)
-            old = top[h]
-            new = jnp.maximum(old, jnp.max(scores, axis=1, keepdims=True))
-            exponent = jnp.exp(scores - new[:, 0:1]) * live
-            scale = jnp.exp(old - new)
-            top[h] = new
-            total[h] = total[h] * scale + jnp.sum(exponent, axis=1, keepdims=True)
-            acc[h] = acc[h] * scale[:, 0:1] + jnp.dot(
-                exponent.astype(jnp.bfloat16), keys[:, 0:512], preferred_element_type=jnp.float32
-            )
+        return lax.rem(y - dy + 4, 4), lax.rem(z - dz + 4, 4)
+
+    def attend(j, half):
+        keys = jnp.concatenate([kv[j, half * 4 + i] for i in range(4)], axis=1)
+        scores = jnp.dot(heads[...], keys, preferred_element_type=jnp.float32) * SCALE
+        scores = (scores.reshape(4, 128, 512) + mask[j, half]).reshape(512, 512)
+        old = top[...]
+        new = jnp.maximum(old, jnp.max(scores, axis=1, keepdims=True))
+        exponent = jnp.exp2(scores - new[:, 0:1])
+        scale = jnp.exp2(old - new)
+        top[...] = new
+        total[...] = total[...] * scale + jnp.sum(exponent, axis=1, keepdims=True)
+        acc[...] = acc[...] * scale[:, 0:1] + lax.dot_general(
+            exponent.astype(jnp.bfloat16), keys[0:512], (((1,), (1,)), ((), ())),
+            preferred_element_type=jnp.float32,
+        )
 
     def gather_copy(half, group, kind, place):
-        low = half * 128 + (64 if kind == 3 else 0)
-        size = 64 if kind >= 2 else 128
+        low = half * 4 + (2 if kind == 3 else 0)
+        size = 2 if kind >= 2 else 4
         on_y = (half == 0) == (group is None)
         to = (at_y if on_y else at_z)(1 if kind % 2 == 0 else 3)
-        block = kv.at[place, pl.ds(low, size)]
+        block = kv.at[place[0], pl.ds(low, size), quarter(place[1])]
         index = 4 if group is None else group
         return pltpu.make_async_remote_copy(
             src_ref=block, dst_ref=block,
@@ -107,10 +140,12 @@
             for kind in (0, 1):
                 gather_copy(half, group, kind, chunk(half, offset, 0)).start()
 
+    keep.wait()
     for copy in sent:
         copy.wait_recv()
     launch(None, 0)
     launch(0, 0)
+    each_far(lambda copy: copy.start())
     keep_w = pltpu.make_async_copy(
         w_down.at[:, pl.ds(pl.multiple_of(s * 896, 896), 896)],
         down_cols.at[pl.ds(pl.multiple_of(s * 256, 256), 256)], w_sem.at[1],
@@ -127,55 +162,45 @@
         )
         copy.start()
         moved.append(copy)
-    attend(e, e)
     for kind in (0, 1):
         offset = 1 if kind == 0 else 3
         for half in (0, 1):
-            gather_copy(half, None, kind, e).wait_recv()
+            gather_copy(half, None, kind, (y, z)).wait_recv()
             gather_copy(half, None, kind + 2, chunk(half, offset, 0)).start()
         launch(kind + 1, offset)
-
-    def near(i, _):
-        offset = 1 + 2 * i
-        attend(chunk(0, offset, 0), chunk(1, offset, 0))
-        return 0
-
-    lax.fori_loop(0, 2, near, 0)
     for half in (0, 1):
         for kind in (2, 3):
-            gather_copy(half, None, kind, e).wait_recv()
+            gather_copy(half, None, kind, (y, z)).wait_recv()
     launch(3, 2)
-    attend(chunk(0, 2, 0), chunk(1, 2, 0))
+    attend(y, 1)
+
+    def take_far(copy):
+        if copy.is_remote:
+            copy.wait_recv()
+        else:
+            copy.wait()
+
+    each_far(take_far)
+    attend(lax.rem(y + 2, 4), 1)
 
     def sides(i, _):
-        offset = offset_of(i)
         for kind in (0, 1):
-            back = 1 if kind == 0 else 3
             for half in (0, 1):
-                gather_copy(half, i, kind, e).wait_recv()
-                gather_copy(half, i, kind + 2, chunk(half, offset, back)).start()
-
-        def both(k, _):
-            attend(chunk(0, offset, 1 + 2 * k), chunk(1, offset, 1 + 2 * k))
-            return 0
-
-        lax.fori_loop(0, 2, both, 0)
+                gather_copy(half, i, kind, (y, z)).wait_recv()
+        attend(chunk(0, offset_of(i), 0)[0], 0)
         return 0
 
     lax.fori_loop(0, 4, sides, 0)
 
-    def far(i, _):
-        offset = offset_of(i)
-        for half in (0, 1):
-            for kind in (2, 3):
-                gather_copy(half, i, kind, e).wait_recv()
-        attend(chunk(0, offset, 2), chunk(1, offset, 2))
+    def last(i, _):
+        attend(lax.rem(y + 1 + 2 * i, 4), 1)
         return 0
 
-    lax.fori_loop(0, 4, far, 0)
+    lax.fori_loop(0, 2, last, 0)
 
     for h in range(4):
-        latent = (acc[h] / total[h][:, 0:1]).astype(jnp.bfloat16)
+        own = pl.ds(h * 128, 128)
+        latent = (acc[own] / total[own, 0:1]).astype(jnp.bfloat16)
         head_out[:, h * 128:(h + 1) * 128] = jnp.dot(
             latent, w_uv[h], preferred_element_type=jnp.float32
         ).astype(jnp.bfloat16)
@@ -255,13 +280,14 @@
         copy.wait_recv()
     for copy in sent + first + second + moved:
         copy.wait_send()
+    each_far(lambda copy: copy.wait_send() if copy.is_remote else None)
     for half in (0, 1):
         for group in range(5):
-            for kind in range(4):
-                gather_copy(half, group if group < 4 else None, kind, e).wait_send()
-
-
-def attend_call(served, queries, chosen, w_uv, w_out, residual, w_down):
+            for kind in range(4 if group == 4 else 2):
+                gather_copy(half, group if group < 4 else None, kind, (y, z)).wait_send()
+
+
+def attend_call(served, served_far, queries, row_slots, w_uv, w_out, residual, w_down):
     vmem = pl.BlockSpec(memory_space=pltpu.VMEM)
     anywhere = pl.BlockSpec(memory_space=pl.ANY)
     bf16, f32 = jnp.bfloat16, jnp.float32
@@ -274,15 +300,15 @@
             jax.ShapeDtypeStruct((32, 1792), bf16),
             jax.ShapeDtypeStruct((2048, 896), bf16),
         ),
-        in_specs=[vmem, vmem, vmem, vmem, anywhere, vmem, anywhere],
+        in_specs=[anywhere, anywhere, vmem, vmem, vmem, anywhere, vmem, anywhere],
         out_specs=(vmem, vmem, anywhere),
         scratch_shapes=[
-            pltpu.VMEM((16, 256, 576), bf16),
-            pltpu.VMEM((4, 128, 576), bf16),
-            pltpu.VMEM((4, 128, 256), f32),
-            pltpu.VMEM((4, 128, 128), f32),
-            pltpu.VMEM((4, 128, 128), f32),
-            pltpu.VMEM((4, 128, 512), f32),
+            pltpu.VMEM((4, 8, 576, 128), bf16),
+            pltpu.VMEM((512, 576), bf16),
+            pltpu.VMEM((4, 2, 128, 512), f32),
+            pltpu.VMEM((512, 128), f32),
+            pltpu.VMEM((512, 128), f32),
+            pltpu.VMEM((512, 512), f32),
             pltpu.VMEM((128, 512), bf16),
             pltpu.VMEM((512, 7168), bf16),
             pltpu.VMEM((2, 16, 16, 1792), bf16),
@@ -290,32 +316,61 @@
             pltpu.VMEM((2, 4, 16, 1792), bf16),
             pltpu.VMEM((2, 3, 16, 1792), bf16),
             pltpu.VMEM((4, 8, 1792), f32),
-            dma((7,)), dma((7,)),
+            dma((2, 7)), dma((2, 7)),
             dma((2, 5, 4)), dma((2, 5, 4)),
             dma((2, 2, 3)), dma((2, 2, 3)),
             dma((7,)), dma((7,)),
-            dma((2,)),
+            dma((4,)),
         ],
         compiler_params=pltpu.CompilerParams(
             collective_id=0, has_side_effects=True, vmem_limit_bytes=56 << 20
         ),
-    )(served, queries, chosen, w_uv, w_out, residual, w_down)
+    )(served, served_far, queries, row_slots, w_uv, w_out, residual, w_down)
+
+
+def serve_kernel(group_passages, passage_place, latents, served, served_far, sem):
+    s, e = lax.axis_index("store"), lax.axis_index("ep")
+    y, z = e // 4, e % 4
+    copies = []
+    for g in range(8):
+        def piece(j, q, dst, i):
+            place = passage_place[group_passages[g * 32 + s * 4 + j]] - s * 32
+            copy = pltpu.make_async_copy(
+                latents.at[place, pl.ds(pl.multiple_of(q * 144, 16), 144)], dst, sem.at[g, i]
+            )
+            copy.start()
+            copies.append(copy)
+
+        piece(y, z, served.at[g], 4)
+        for i in range(4):
+            piece(
+                jnp.where(s < 4, i, lax.rem(y + 2, 4)), jnp.where(s < 4, lax.rem(z + 2, 4), i),
+                served_far.at[g, i], i,
+            )
+    for copy in copies:
+        copy.wait()
 
 
 def serve(latent_store, group_passages, passage_place):
-    s, e = lax.axis_index("store"), lax.axis_index("ep")
-    lists = group_passages.reshape(8, 8, 4)
-    ids = lax.dynamic_slice(lists, (0, s, e // 4), (8, 1, 1)).reshape(8)
-    places = passage_place[ids] - s * 32
-    return jax.vmap(
-        lambda row: lax.dynamic_slice(latent_store, (row, (e % 4) * 32, 0), (1, 32, 576))[0]
-    )(places)
+    smem = pl.BlockSpec(memory_space=pltpu.SMEM)
+    vmem = pl.BlockSpec(memory_space=pltpu.VMEM)
+    anywhere = pl.BlockSpec(memory_space=pl.ANY)
+    return pl.pallas_call(
+        serve_kernel,
+        name="serve",
+        out_shape=(
+            jax.ShapeDtypeStruct((8, 144, 128), jnp.bfloat16),
+            jax.ShapeDtypeStruct((8, 4, 144, 128), jnp.bfloat16),
+        ),
+        in_specs=[smem, smem, anywhere],
+        out_specs=(vmem, vmem),
+        scratch_shapes=[pltpu.SemaphoreType.DMA((8, 5))],
+    )(group_passages, passage_place, jnp.swapaxes(latent_store, 1, 2))
 
 
 def front(queries, residual_in, latent_store, group_passages, row_slots, passage_place, w_uv, w_out, w_down):
-    served = serve(latent_store, group_passages, passage_place)
-    chosen = jnp.any(row_slots[:, :, None] == jnp.arange(32, dtype=jnp.int32), axis=1).astype(jnp.bfloat16)
-    return attend_call(served, queries, chosen, w_uv, w_out, residual_in, w_down[0])
+    served, served_far = serve(latent_store, group_passages, passage_place)
+    return attend_call(served, served_far, queries, row_slots.T, w_uv, w_out, residual_in, w_down[0])
 
 
 def expert_kernel(

time: 188 us -> 168 us (0.89)
  local copies, waits for them, and re-layouts: 18.1 us -> 3.68 us
  Pallas kernels: 167 us -> 163 us
    pallas_call x1, Pallas kernels: 78.8 us -> 69.3 us  [attend_call(): pl.pallas_call(attend_kernel, name='attend', out_shape=(jax.ShapeDtypeStr...]
    unnamed x10 -> x5, local copies, waits for them, and re-layouts: 10.5 us -> 1.56 us
    gather x3 -> x0, local copies, waits for them, and re-layouts: 3.65 us -> none  [the longest x2 3 us: serve(): lax.dynamic_slice(latent_store, (row, e % 4 * 32, 0), (1, 32, 576))[0]]
    pallas_call x0 -> x1, Pallas kernels: none -> 3.58 us  [serve(): pl.pallas_call(serve_kernel, name='serve', out_shape=(jax.ShapeDtypeStruc...]
where the time goes in v3:
time: 168 us; the launch traced here: 167 us
  Pallas kernels  163 us (97%)
  local copies, waits for them, and re-layouts  3.68 us (2%)
    pallas_call x1, Pallas kernels, expert_call(): pl.pallas_call(expert_kernel, name='experts', out_shape=jax.ShapeDtypeStr...  89.8 us
    pallas_call x1, Pallas kernels, attend_call(): pl.pallas_call(attend_kernel, name='attend', out_shape=(jax.ShapeDtypeStr...  69.3 us
    pallas_call x1, Pallas kernels, serve(): pl.pallas_call(serve_kernel, name='serve', out_shape=(jax.ShapeDtypeStruc...  3.58 us

profile of v3, /device:TPU:1, one launch (start us, length us, event | category | flops | bytes accessed | tf_op | source)
XLA Modules:
  0.0 167.2 jit_solution(1705724375930339094)
XLA Ops:
  0.0 3.6 %serve.1 = (bf16[8,144,128]{2,1,0:T(8,128)(2,1)}, bf16[8,4,144,128]{3,2,1,0:T(8,128)(2,1)}) custom-call(s32[256]{0:T(256)} %group_passages.1, s32[256]{0:T(256)} %passage_place.1, bf16[32,576,128]{2,1,0:T(8,128)(2,1)} %bitcast.11), custom_call_target="tpu_custom_call" | custom-call | tf_op jit(solution)/shard_map/serve/pallas_call | solution.py:358
  3.6 0.0 copy-start
  3.6 0.0 copy-start.1
  3.6 69.3 %attend.1 = (f32[8,7168]{1,0:T(8,128)}, bf16[32,1792]{1,0:T(8,128)(2,1)}, bf16[2048,896]{1,0:T(8,128)(2,1)}) custom-call(bf16[8,144,128]{2,1,0:T(8,128)(2,1)} %get-tuple-element.10.served, bf16[8,4,144,128]{3,2,1,0:T(8,128)(2,1)} %get-tuple-element.11.served_far, bf16[128,2304]{1,0:T(8,128)(2,1)} %queries.1, s32[16,128]{1,0:T(8,128)} %bitcast.15, ...), custom_call_target="tpu_custom_call" | custom-call | tf_op jit(solution)/shard_map/attend/pallas_call | solution.py:295
  72.9 0.0 copy-done
  73.0 0.0 copy-done.1
  73.0 0.1 select_reduce_fusion
  73.1 0.1 copy.24
  73.2 0.1 copy.23
  73.3 0.1 copy.22
  73.4 0.2 fusion.1
  73.6 0.8 convert_element_type.56.place
  74.4 0.1 copy.27
  74.5 0.3 fusion
  74.8 0.3 convert_element_type.62
  75.1 0.7 copy.28.weigh
  75.8 89.8 %experts.1 = bf16[8,7168]{1,0:T(8,128)(2,1)} custom-call(bf16[32,1792]{1,0:T(8,128)(2,1)} %get-tuple-element.12.normed, f32[8,7168]{1,0:T(8,128)} %get-tuple-element.13.mixed, bf16[256,32]{1,0:T(8,128)(2,1)} %convert_element_type.56.place, bf16[2,32,256]{2,1,0:T(8,128)(2,1)} %copy.28.weigh, bf16[7168,256]{1,0:T(8,128)(2,1)} %bitcast.13, ...), custom_call_target="tpu_custom_call" | custom-call | tf_op jit(solution)/shard_map/experts/pallas_call | solution.py:600
  165.6 1.6 copy.30
  (7 shorter events, 0.1 us)
Async XLA Ops:
  3.6 69.4 %copy-start = (f32[8,4]{0,1:T(4,128)S(1)}, f32[8,4]{0,1:T(4,128)}, u32[]{:S(2)}) copy-start(f32[8,4]{0,1:T(4,128)} %param.22) | copy-start | bytes 388
  3.6 69.4 %copy-start.1 = (s32[8,4]{0,1:T(4,128)S(1)}, s32[8,4]{0,1:T(4,128)}, u32[]{:S(2)}) copy-start(s32[8,4]{0,1:T(4,128)} %param.21) | copy-start | bytes 388

commit v4 on v3

v4 whole, which is shorter than its diff:
```python
import functools

import jax
import jax.numpy as jnp
from jax import lax
from jax.experimental import pallas as pl
from jax.experimental.pallas import tpu as pltpu
from jax.sharding import PartitionSpec as P

SCALE = 192.0 ** (-0.5) * 1.4426950408889634
MESH = pl.DeviceIdType.MESH
LOW = -1e29
FAR_LOW = 1e30


def offset_of(i):
    return i + i // 2 - 2 * (i // 3)


def layer_kernel(
    served, served_far, queries, row_slots, w_uv, w_out, residual, ids, gates, w_gate, w_up, w_down,
    out,
    kv, heads, mask, top, total, acc, head_out, out_w, part, part_in, summed, summed_in, rows,
    table, weigh, normed, outgoing, arrived, x_rows, in_w, down_w, pre, hid, y_part, returned, mix_out, mix_in,
    x_send, x_recv, g_send, g_recv, r_send, r_recv, d_send, d_recv, w_sem,
    n_send, n_recv, t_send, t_recv, a_send, a_recv, h_send, h_recv, b_send, b_recv, m_send, m_recv,
):
    s = lax.axis_index("store")
    e = lax.axis_index("ep")
    y, z = e // 4, e % 4

    def at_y(d):
        return (s, lax.rem(y + d, 4) * 4 + z)

    def at_z(d):
        return (s, y * 4 + lax.rem(z + d, 4))

    def at_s(d):
        return (lax.rem(s + d, 8), e)

    def quarter(q):
        return pl.ds(pl.multiple_of(q * 144, 16), 144)

    sibling = s + 1 - 2 * (s % 2)

    def on_ep(dy, dz):
        return lax.rem(y + dy, 4) * 4 + lax.rem(z + dz, 4)

    peers = [at_s(d) for d in range(1, 8)]
    peers += [(s, on_ep(dy, dz)) for dy in range(4) for dz in range(4) if dy or dz]
    barrier = pltpu.get_barrier_semaphore()
    for peer in peers:
        pl.semaphore_signal(barrier, inc=1, device_id=peer, device_id_type=MESH)
    get_w = pltpu.make_async_copy(w_out, out_w, w_sem.at[0])
    get_in = [
        pltpu.make_async_copy(w_gate, in_w.at[:, 0:256], w_sem.at[4]),
        pltpu.make_async_copy(w_up, in_w.at[:, 256:512], w_sem.at[5]),
    ]
    for load in [get_w] + get_in:
        load.start()

    lane_row = lax.broadcasted_iota(jnp.int32, (8, 128), 1) % 8
    repeat = (lax.broadcasted_iota(jnp.int32, (8, 128), 0) == lane_row).astype(jnp.float32)
    wide_ids = jnp.dot(ids[...].astype(jnp.float32), repeat, preferred_element_type=jnp.float32)
    wide_gates = jnp.dot(
        gates[...], repeat, preferred_element_type=jnp.float32, precision=lax.Precision.HIGHEST
    )
    pair = lax.broadcasted_iota(jnp.int32, (64, 128), 0)
    expert = (pair // 4).astype(jnp.float32)
    routed = jnp.zeros((64, 128), jnp.float32)
    gate = jnp.zeros((64, 128), jnp.float32)
    for i in range(4):
        named = (wide_ids[i:i + 1] == expert).astype(jnp.float32)
        routed = routed + named
        gate = gate + named * wide_gates[i:i + 1]
    before = lax.broadcasted_iota(jnp.int32, (128, 128), 0)
    upto = lax.broadcasted_iota(jnp.int32, (128, 128), 1) % 8
    earlier = jnp.dot(
        routed.astype(jnp.bfloat16), (before < upto).astype(jnp.bfloat16), preferred_element_type=jnp.float32
    )
    table[s] = jnp.where((routed > 0.5) & (earlier == (pair % 4).astype(jnp.float32)), gate, 0.0)
    pl.semaphore_wait(barrier, len(peers))

    sent = []
    for d in range(1, 8):
        to = at_s(d)
        copy = pltpu.make_async_remote_copy(
            src_ref=served.at[to[0]], dst_ref=kv.at[y, s, quarter(z)],
            send_sem=x_send.at[0, d - 1], recv_sem=x_recv.at[0, d - 1],
            device_id=to, device_id_type=MESH,
        )
        copy.start()
        sent.append(copy)
    keep = pltpu.make_async_copy(served.at[s], kv.at[y, s, quarter(z)], w_sem.at[2])
    keep.start()

    def copy_to(src, dst, send, recv, device):
        return pltpu.make_async_remote_copy(
            src_ref=src, dst_ref=dst, send_sem=send, recv_sem=recv, device_id=device, device_id_type=MESH
        )

    def far_copies(whole):
        def target(ref):
            return ref.at[lax.rem(y + 2, 4), s] if whole else ref.at[:, s, quarter(lax.rem(z + 2, 4))]

        def source(g):
            return served_far.at[g].reshape(576, 128) if whole else served_far.at[g]

        return [
            pltpu.make_async_remote_copy(
                src_ref=source(at_s(d)[0]), dst_ref=target(kv),
                send_sem=x_send.at[1, d - 1], recv_sem=x_recv.at[1, d - 1],
                device_id=at_s(d), device_id_type=MESH,
            )
            for d in range(1, 8)
        ] + [pltpu.make_async_copy(source(s), target(kv), w_sem.at[3])]

    def each_far(act):
        for whole in (False, True):
            @pl.when((s >= 4) if whole else (s < 4))
            def _():
                for copy in far_copies(whole):
                    act(copy)

    for h in range(4):
        heads[h * 128:(h + 1) * 128] = queries[:, h * 576:(h + 1) * 576]
    slot = lax.broadcasted_iota(jnp.int32, (32, 128), 0)
    chosen = jnp.zeros((32, 128), jnp.bool_)
    for i in range(16):
        chosen = chosen | (row_slots[i:i + 1] == slot)
    chosen = chosen.astype(jnp.bfloat16)
    slot_row = lax.broadcasted_iota(jnp.int32, (32, 512), 0)
    token_col = lax.broadcasted_iota(jnp.int32, (32, 512), 1)
    for j in range(4):
        for half in (0, 1):
            spread = (slot_row == (token_col // 128 + 4 * half) * 4 + j).astype(jnp.bfloat16)
            live = lax.dot_general(
                chosen, spread, (((0,), (0,)), ((), ())), preferred_element_type=jnp.float32
            )
            mask[j, half] = (live - 1.0) * FAR_LOW
    top[...] = jnp.full_like(top, LOW)
    total[...] = jnp.zeros_like(total)
    acc[...] = jnp.zeros_like(acc)

    def chunk(half, first, second):
        dy, dz = (first, second) if half == 0 else (second, first)
        return lax.rem(y - dy + 4, 4), lax.rem(z - dz + 4, 4)

    def attend(j, half):
        keys = jnp.concatenate([kv[j, half * 4 + i] for i in range(4)], axis=1)
        scores = jnp.dot(heads[...], keys, preferred_element_type=jnp.float32) * SCALE
        scores = (scores.reshape(4, 128, 512) + mask[j, half]).reshape(512, 512)
        old = top[...]
        new = jnp.maximum(old, jnp.max(scores, axis=1, keepdims=True))
        exponent = jnp.exp2(scores - new[:, 0:1])
        scale = jnp.exp2(old - new)
        top[...] = new
        total[...] = total[...] * scale + jnp.sum(exponent, axis=1, keepdims=True)
        acc[...] = acc[...] * scale[:, 0:1] + lax.dot_general(
            exponent.astype(jnp.bfloat16), keys[0:512], (((1,), (1,)), ((), ())),
            preferred_element_type=jnp.float32,
        )

    def build_weigh():
        lane = lax.broadcasted_iota(jnp.int32, (64, 128), 1)
        gated = jnp.concatenate([jnp.where(lane // 8 == g, table[g], 0.0) for g in range(8)], axis=0)
        from_row = lax.broadcasted_iota(jnp.int32, (512, 512), 0)
        to_col = lax.broadcasted_iota(jnp.int32, (512, 512), 1)
        place = (to_col // 4 % 8) * 64 + (to_col // 32) * 4 + to_col % 4
        move = (from_row == place).astype(jnp.bfloat16)
        high = gated.astype(jnp.bfloat16)
        low = (gated - high.astype(jnp.float32)).astype(jnp.bfloat16)
        for i, held in ((0, high), (1, low)):
            weigh[i] = lax.dot_general(
                held, move, (((0,), (0,)), ((), ())), preferred_element_type=jnp.float32
            )[0:64].astype(jnp.bfloat16)

    def gather_copy(half, group, kind, place):
        low = half * 4 + (2 if kind == 3 else 0)
        size = 2 if kind >= 2 else 4
        on_y = (half == 0) == (group is None)
        to = (at_y if on_y else at_z)(1 if kind % 2 == 0 else 3)
        block = kv.at[place[0], pl.ds(low, size), quarter(place[1])]
        index = 4 if group is None else group
        return pltpu.make_async_remote_copy(
            src_ref=block, dst_ref=block,
            send_sem=g_send.at[half, index, kind], recv_sem=g_recv.at[half, index, kind],
            device_id=to, device_id_type=MESH,
        )

    def launch(group, offset):
        for half in (0, 1):
            for kind in (0, 1):
                gather_copy(half, group, kind, chunk(half, offset, 0)).start()

    keep.wait()
    for copy in sent:
        copy.wait_recv()
    launch(None, 0)
    launch(0, 0)
    tables = []
    for d in range(1, 8):
        copy = pltpu.make_async_remote_copy(
            src_ref=table.at[s], dst_ref=table.at[s], send_sem=n_send.at[d], recv_sem=n_recv.at[d],
            device_id=at_s(d), device_id_type=MESH,
        )
        copy.start()
        tables.append(copy)
    each_far(lambda copy: copy.start())
    keep_w = pltpu.make_async_copy(
        w_down.at[:, pl.ds(pl.multiple_of(s * 896, 896), 896)],
        down_w.at[pl.ds(pl.multiple_of(s * 256, 256), 256)], w_sem.at[1],
    )
    keep_w.start()
    moved = []
    for d in range(1, 8):
        to = at_s(d)
        copy = pltpu.make_async_remote_copy(
            src_ref=w_down.at[:, pl.ds(pl.multiple_of(to[0] * 896, 896), 896)],
            dst_ref=down_w.at[pl.ds(pl.multiple_of(s * 256, 256), 256)],
            send_sem=d_send.at[d - 1], recv_sem=d_recv.at[d - 1],
            device_id=to, device_id_type=MESH,
        )
        copy.start()
        moved.append(copy)
    for kind in (0, 1):
        offset = 1 if kind == 0 else 3
        for half in (0, 1):
            gather_copy(half, None, kind, (y, z)).wait_recv()
            gather_copy(half, None, kind + 2, chunk(half, offset, 0)).start()
        launch(kind + 1, offset)
    for half in (0, 1):
        for kind in (2, 3):
            gather_copy(half, None, kind, (y, z)).wait_recv()
    launch(3, 2)
    for copy in tables:
        copy.wait_recv()
    build_weigh()
    attend(y, 1)

    def take_far(copy):
        if copy.is_remote:
            copy.wait_recv()
        else:
            copy.wait()

    each_far(take_far)
    attend(lax.rem(y + 2, 4), 1)

    def sides(i, _):
        for kind in (0, 1):
            for half in (0, 1):
                gather_copy(half, i, kind, (y, z)).wait_recv()
        attend(chunk(0, offset_of(i), 0)[0], 0)
        return 0

    lax.fori_loop(0, 4, sides, 0)

    def last(i, _):
        attend(lax.rem(y + 1 + 2 * i, 4), 1)
        return 0

    lax.fori_loop(0, 2, last, 0)

    for h in range(4):
        own = pl.ds(h * 128, 128)
        latent = (acc[own] / total[own, 0:1]).astype(jnp.bfloat16)
        head_out[:, h * 128:(h + 1) * 128] = jnp.dot(
            latent, w_uv[h], preferred_element_type=jnp.float32
        ).astype(jnp.bfloat16)
    get_w.wait()

    first = []
    for half in (0, 1):
        def project(t, _):
            lane = pl.multiple_of(t * 256, 256)
            both = []
            for k in (0, 1):
                column = pl.multiple_of(half * 3584 + k * 1792 + t * 256, 256)
                both.append(jnp.dot(
                    head_out[...], out_w[:, pl.ds(column, 256)], preferred_element_type=jnp.float32
                ).reshape(16, 8, 256))
            tile = jnp.concatenate(both, axis=1).astype(jnp.bfloat16)
            if half == 0:
                part[0, :, :, pl.ds(lane, 256)] = tile
            else:
                for p in range(16):
                    part[1, (p % 4) * 4 + p // 4, :, pl.ds(lane, 256)] = tile[p]
            return 0

        lax.fori_loop(0, 7, project, 0)
        for d in (1, 2, 3):
            to, line = (at_y(d), lax.rem(y + d, 4)) if half == 0 else (at_z(d), lax.rem(z + d, 4))
            copy = pltpu.make_async_remote_copy(
                src_ref=part.at[half, pl.ds(line * 4, 4)], dst_ref=part_in.at[half, d - 1],
                send_sem=r_send.at[half, 0, d - 1], recv_sem=r_recv.at[half, 0, d - 1],
                device_id=to, device_id_type=MESH,
            )
            copy.start()
            first.append(copy)
    second = []
    for half in (0, 1):
        for d in (1, 2, 3):
            first[half * 3 + d - 1].wait_recv()
        own = y if half == 0 else z

        def add(k, _):
            value = part[half, own * 4 + k].astype(jnp.float32)
            for d in range(3):
                value = value + part_in[half, d, k].astype(jnp.float32)
            summed[half, k] = value.astype(jnp.bfloat16)
            return 0

        lax.fori_loop(0, 4, add, 0)
        for d in (1, 2, 3):
            to, line = (at_z(d), lax.rem(z + d, 4)) if half == 0 else (at_y(d), lax.rem(y + d, 4))
            copy = pltpu.make_async_remote_copy(
                src_ref=summed.at[half, line], dst_ref=summed_in.at[half, d - 1],
                send_sem=r_send.at[half, 1, d - 1], recv_sem=r_recv.at[half, 1, d - 1],
                device_id=to, device_id_type=MESH,
            )
            copy.start()
            second.append(copy)
    squares = jnp.zeros((8, 1), jnp.float32)
    for half in (0, 1):
        for d in (1, 2, 3):
            second[half * 3 + d - 1].wait_recv()
        value = summed[half, z if half == 0 else y].astype(jnp.float32)
        for d in range(3):
            value = value + summed_in[half, d].astype(jnp.float32)
        for k in (0, 1):
            q = 2 * half + k
            row = residual[:, q * 1792:(q + 1) * 1792].astype(jnp.float32) + value[k * 8:(k + 1) * 8]
            rows[q] = row
            squares = squares + jnp.sum(row * row, axis=1, keepdims=True)
    norm = lax.rsqrt(squares / 7168.0 + 1e-06)
    for q in (0, 2):
        two = jnp.concatenate([rows[q] * norm, rows[q + 1] * norm], axis=0)
        normed[0, q * 8:(q + 2) * 8] = two.astype(jnp.bfloat16)

    swap = copy_to(normed.at[0], normed.at[1], n_send.at[0], n_recv.at[0], at_s(4))
    swap.start()

    def dispatch(side, k, dz):
        to = on_ep(offset_of(k), dz)
        return copy_to(
            outgoing.at[side, to], arrived.at[side, e], t_send.at[side, k, dz], t_recv.at[side, k, dz], (s, to)
        )

    def give_back(k, dz):
        to = on_ep(4 - offset_of(k), dz)
        return copy_to(y_part.at[k, lax.rem(z + dz, 4)], returned.at[e], b_send.at[k, dz], b_recv.at[k, dz], (s, to))

    def gather(k, kind):
        to = at_s((2, 6)[kind]) if kind < 2 else (sibling, e)
        block = lax.rem(s + (0, 0, 0, 4, 6, 2)[kind], 8)
        ref = x_rows.at[k, pl.ds(pl.multiple_of(block * 16, 16), 16)]
        return copy_to(ref, ref, a_send.at[k, kind], a_recv.at[k, kind], to)

    def share(k, kind):
        to = at_s((2, 6, 4)[kind]) if kind < 3 else (sibling, e)
        block = lax.rem(s + (0, 0, 0, 0, 6, 2, 4)[kind], 8)
        ref = hid.at[k, :, pl.ds(pl.multiple_of(block * 256, 256), 256)]
        return copy_to(ref, ref, h_send.at[k, kind], h_recv.at[k, kind], to)

    def spread_rows(side):
        group = lax.rem(s + 4 * side, 8)
        to_row = lax.broadcasted_iota(jnp.int32, (256, 64), 0)
        from_pair = lax.broadcasted_iota(jnp.int32, (256, 64), 1)
        widen = (from_pair == (to_row // 16) * 4 + to_row % 4).astype(jnp.bfloat16)
        held = jnp.dot(
            widen, (table[group] > 0).astype(jnp.bfloat16), preferred_element_type=jnp.float32
        )[:, 0:32]
        row_quarter = lax.broadcasted_iota(jnp.int32, (256, 32), 0) // 4 % 4
        col_quarter = lax.broadcasted_iota(jnp.int32, (256, 32), 1) // 8
        place = jnp.where(row_quarter == col_quarter, held, 0.0).astype(jnp.bfloat16)
        outgoing[side] = jnp.dot(
            place, normed[side], preferred_element_type=jnp.float32
        ).astype(jnp.bfloat16).reshape(16, 16, 1792)
        arrived[side, e] = outgoing[side, e]

    def send_rows(side, k):
        for dz in (0, 1, 3, 2):
            if k or dz:
                dispatch(side, k, dz).start()

    spread_rows(0)
    send_rows(0, 0)
    send_rows(0, 1)
    swap.wait_recv()
    spread_rows(1)
    for side, k in ((1, 0), (0, 2), (1, 1), (0, 3), (1, 2), (1, 3)):
        send_rows(side, k)

    rows16 = lax.broadcasted_iota(jnp.int32, (16, 64), 0)
    cols64 = lax.broadcasted_iota(jnp.int32, (16, 64), 1)

    def enter(side, k):
        for dz in range(1, 4):
            dispatch(side, k, dz).wait_recv()

        @pl.when(k > 0)
        def _():
            dispatch(side, k, 0).wait_recv()

        line = lax.rem(y + 4 - offset_of(k), 4)
        block = arrived[side, pl.ds(line * 4, 4)].reshape(64, 1792)
        low = pl.multiple_of(lax.rem(s + 4 * side, 8) * 16, 16)
        for q in range(4):
            take = (cols64 == (rows16 // 4) * 16 + q * 4 + rows16 % 4).astype(jnp.bfloat16)
            x_rows[k, pl.ds(low, 16), q * 1792:(q + 1) * 1792] = jnp.dot(
                take, block, preferred_element_type=jnp.float32
            ).astype(jnp.bfloat16)
        for kind in ((0, 1, 2), (3,))[side]:
            gather(k, kind).start()

    def pass_on(k):
        for kind in (0, 1):
            gather(k, kind).wait_recv()
            gather(k, kind + 4).start()

    def hidden(k):
        for kind in range(2, 6):
            gather(k, kind).wait_recv()
        pre[...] = jnp.zeros_like(pre)

        def add(q, _):
            low = pl.multiple_of(q * 1792, 1792)
            pre[...] += jnp.dot(
                x_rows[k, :, pl.ds(low, 1792)], in_w[pl.ds(low, 1792)], preferred_element_type=jnp.float32
            )
            return 0

        lax.fori_loop(0, 4, add, 0)
        gate = pre[:, 0:256]
        hid[k, :, pl.ds(pl.multiple_of(s * 256, 256), 256)] = (
            gate / (1.0 + jnp.exp(-gate)) * pre[:, 256:512]
        ).astype(jnp.bfloat16)
        for kind in range(4):
            share(k, kind).start()

    to128 = lax.broadcasted_iota(jnp.int32, (128, 128), 0)
    from128 = lax.broadcasted_iota(jnp.int32, (128, 128), 1)

    def project(k):
        for kind in range(3):
            share(k, kind).wait_recv()
            share(k, kind + 4).start()
        for kind in range(3, 7):
            share(k, kind).wait_recv()
        value = jnp.dot(hid[k], down_w[...], preferred_element_type=jnp.float32).astype(jnp.bfloat16)
        order = (from128 == (to128 // 4 % 8) * 16 + (to128 // 32) * 4 + to128 % 4).astype(jnp.bfloat16)
        y_part[k] = jnp.dot(order, value, preferred_element_type=jnp.float32).astype(jnp.bfloat16).reshape(4, 32, 896)
        for dz in range(1, 4):
            give_back(k, dz).start()

        @pl.when(k > 0)
        def _():
            give_back(k, 0).start()

        @pl.when(k == 0)
        def _():
            returned[e] = y_part[k, z]

    def step(t, _):
        @pl.when(t < 4)
        def _():
            enter(0, t)

        @pl.when(t == 1)
        def _():
            for load in get_in:
                load.wait()

        @pl.when((t >= 1) & (t < 5))
        def _():
            hidden(t - 1)

        @pl.when(t < 4)
        def _():
            enter(1, t)
            pass_on(t)

        @pl.when(t == 2)
        def _():
            keep_w.wait()
            for copy in moved:
                copy.wait_recv()

        @pl.when(t >= 2)
        def _():
            project(t - 2)

        return 0

    lax.fori_loop(0, 6, step, 0)

    for k in range(4):
        for dz in range(4):
            if k or dz:
                give_back(k, dz).wait_recv()
    back = returned[...].reshape(512, 896)
    mix_out[...] = jnp.dot(weigh[0], back, preferred_element_type=jnp.float32) + jnp.dot(
        weigh[1], back, preferred_element_type=jnp.float32
    )
    columns = pl.ds(pl.multiple_of(s * 896, 896), 896)
    handed = []
    for d in (4, 2, 6, 3, 5, 1, 7):
        to = at_s(d)
        copy = copy_to(
            mix_out.at[pl.ds(pl.multiple_of(to[0] * 8, 8), 8)], mix_in.at[:, columns],
            m_send.at[d - 1], m_recv.at[d - 1], to,
        )
        copy.start()
        handed.append(copy)
    mix_in[:, columns] = mix_out[pl.ds(pl.multiple_of(s * 8, 8), 8)]
    for copy in handed:
        copy.wait_recv()
    for q in range(4):
        own = slice(q * 1792, (q + 1) * 1792)
        out[:, own] = (rows[q] + mix_in[:, own]).astype(jnp.bfloat16)

    for copy in handed + tables + [swap] + moved:
        copy.wait_send()
    for k in range(4):
        for dz in range(4):
            if k or dz:
                dispatch(0, k, dz).wait_send()
                dispatch(1, k, dz).wait_send()
                give_back(k, dz).wait_send()
        for kind in range(6):
            gather(k, kind).wait_send()
        for kind in range(7):
            share(k, kind).wait_send()
    for copy in sent + first + second:
        copy.wait_send()
    each_far(lambda copy: copy.wait_send() if copy.is_remote else None)
    for half in (0, 1):
        for group in range(5):
            for kind in range(4 if group == 4 else 2):
                gather_copy(half, group if group < 4 else None, kind, (y, z)).wait_send()


def layer_call(*arrays):
    vmem = pl.BlockSpec(memory_space=pltpu.VMEM)
    anywhere = pl.BlockSpec(memory_space=pl.ANY)
    bf16, f32 = jnp.bfloat16, jnp.float32
    dma = pltpu.SemaphoreType.DMA
    return pl.pallas_call(
        layer_kernel,
        name="layer",
        out_shape=jax.ShapeDtypeStruct((8, 7168), bf16),
        in_specs=[anywhere, anywhere, vmem, vmem, vmem, anywhere, vmem, vmem, vmem, anywhere, anywhere, anywhere],
        out_specs=vmem,
        scratch_shapes=[
            pltpu.VMEM((4, 8, 576, 128), bf16),
            pltpu.VMEM((512, 576), bf16),
            pltpu.VMEM((4, 2, 128, 512), f32),
            pltpu.VMEM((512, 128), f32),
            pltpu.VMEM((512, 128), f32),
            pltpu.VMEM((512, 512), f32),
            pltpu.VMEM((128, 512), bf16),
            pltpu.VMEM((512, 7168), bf16),
            pltpu.VMEM((2, 16, 16, 1792), bf16),
            pltpu.VMEM((2, 3, 4, 16, 1792), bf16),
            pltpu.VMEM((2, 4, 16, 1792), bf16),
            pltpu.VMEM((2, 3, 16, 1792), bf16),
            pltpu.VMEM((4, 8, 1792), f32),
            pltpu.VMEM((8, 64, 128), f32),
            pltpu.VMEM((2, 64, 512), bf16),
            pltpu.VMEM((2, 32, 1792), bf16),
            pltpu.VMEM((2, 16, 16, 1792), bf16),
            pltpu.VMEM((2, 16, 16, 1792), bf16),
            pltpu.VMEM((4, 128, 7168), bf16),
            pltpu.VMEM((7168, 512), bf16),
            pltpu.VMEM((2048, 896), bf16),
            pltpu.VMEM((128, 512), f32),
            pltpu.VMEM((4, 128, 2048), bf16),
            pltpu.VMEM((4, 4, 32, 896), bf16),
            pltpu.VMEM((16, 32, 896), bf16),
            pltpu.VMEM((64, 896), f32),
            pltpu.VMEM((8, 7168), f32),
            dma((2, 7)), dma((2, 7)),
            dma((2, 5, 4)), dma((2, 5, 4)),
            dma((2, 2, 3)), dma((2, 2, 3)),
            dma((7,)), dma((7,)),
            dma((6,)),
            dma((8,)), dma((8,)),
            dma((2, 4, 4)), dma((2, 4, 4)),
            dma((4, 6)), dma((4, 6)),
            dma((4, 7)), dma((4, 7)),
            dma((4, 4)), dma((4, 4)),
            dma((7,)), dma((7,)),
        ],
        compiler_params=pltpu.CompilerParams(
            collective_id=0, has_side_effects=True, vmem_limit_bytes=60 << 20
        ),
    )(*arrays)


def serve_kernel(group_passages, passage_place, latents, served, served_far, sem):
    s, e = lax.axis_index("store"), lax.axis_index("ep")
    y, z = e // 4, e % 4
    copies = []
    for g in range(8):
        def piece(j, q, dst, i):
            place = passage_place[group_passages[g * 32 + s * 4 + j]] - s * 32
            copy = pltpu.make_async_copy(
                latents.at[place, pl.ds(pl.multiple_of(q * 144, 16), 144)], dst, sem.at[g, i]
            )
            copy.start()
            copies.append(copy)

        piece(y, z, served.at[g], 4)
        for i in range(4):
            piece(
                jnp.where(s < 4, i, lax.rem(y + 2, 4)), jnp.where(s < 4, lax.rem(z + 2, 4), i),
                served_far.at[g, i], i,
            )
    for copy in copies:
        copy.wait()


def serve(latent_store, group_passages, passage_place):
    smem = pl.BlockSpec(memory_space=pltpu.SMEM)
    vmem = pl.BlockSpec(memory_space=pltpu.VMEM)
    anywhere = pl.BlockSpec(memory_space=pl.ANY)
    return pl.pallas_call(
        serve_kernel,
        name="serve",
        out_shape=(
            jax.ShapeDtypeStruct((8, 144, 128), jnp.bfloat16),
            jax.ShapeDtypeStruct((8, 4, 144, 128), jnp.bfloat16),
        ),
        in_specs=[smem, smem, anywhere],
        out_specs=(vmem, vmem),
        scratch_shapes=[pltpu.SemaphoreType.DMA((8, 5))],
    )(group_passages, passage_place, jnp.swapaxes(latent_store, 1, 2))


def body(
    queries, residual_in, latent_store, group_passages, row_slots, passage_place, w_uv, w_out,
    expert_ids, expert_gates, w_gate, w_up, w_down,
):
    served, served_far = serve(latent_store, group_passages, passage_place)
    return layer_call(
        served, served_far, queries, row_slots.T, w_uv, w_out, residual_in,
        expert_ids.T, expert_gates.T, w_gate[0], w_up[0], w_down[0],
    )


def solution(mesh):
    return jax.shard_map(
        body,
        mesh=mesh,
        in_specs=(
            P("store", "ep"),
            P(("store", "ep"), None),
            P("store", None, None),
            P(),
            P("store", None),
            P(),
            P("ep", None, None),
            P("ep", None),
            P(("store", "ep"), None),
            P(("store", "ep"), None),
            P("ep", None, "store"),
            P("ep", None, "store"),
            P("ep", "store", None),
        ),
        out_specs=P(("store", "ep"), None),
        check_vma=False,
    )
```

time: 168 us -> 145 us (0.86)
  Pallas kernels: 163 us -> 143 us
  local copies, waits for them, and re-layouts: 3.68 us -> 1.55 us
    pallas_call x2 -> x1, Pallas kernels: 159 us -> 139 us  [layer_call(): pl.pallas_call(layer_kernel, name='layer', out_shape=jax.ShapeDtypeStruct...]
    convert_element_type x3 -> x0, local copies, waits for them, and re-layouts: 1.79 us -> none  [the longest x2 0.99 us: routing(): jnp.einsum('nrec,qp->nqrepc', weigh, eye).reshape(2, 32, 256)]
where the time goes in v4:
time: 145 us; the launch traced here: 144 us
  Pallas kernels  143 us (99%)
  local copies, waits for them, and re-layouts  1.55 us (1%)
    pallas_call x1, Pallas kernels, layer_call(): pl.pallas_call(layer_kernel, name='layer', out_shape=jax.ShapeDtypeStruct...  139 us
    pallas_call x1, Pallas kernels, serve(): pl.pallas_call(serve_kernel, name='serve', out_shape=(jax.ShapeDtypeStruc...  3.72 us

profile of v4, /device:TPU:1, one launch (start us, length us, event | category | flops | bytes accessed | tf_op | source)
XLA Modules:
  0.0 144.4 jit_solution(8227127938486543572)
XLA Ops:
  0.0 3.7 %serve.1 = (bf16[8,144,128]{2,1,0:T(8,128)(2,1)}, bf16[8,4,144,128]{3,2,1,0:T(8,128)(2,1)}) custom-call(s32[256]{0:T(256)} %group_passages.1, s32[256]{0:T(256)} %passage_place.1, bf16[32,576,128]{2,1,0:T(8,128)(2,1)} %bitcast.7), custom_call_target="tpu_custom_call" | custom-call | tf_op jit(solution)/shard_map/serve/pallas_call | solution.py:628
  3.7 139.1 %layer.1 = bf16[8,7168]{1,0:T(8,128)(2,1)} custom-call(bf16[8,144,128]{2,1,0:T(8,128)(2,1)} %get-tuple-element.7.served, bf16[8,4,144,128]{3,2,1,0:T(8,128)(2,1)} %get-tuple-element.8.served_far, bf16[128,2304]{1,0:T(8,128)(2,1)} %queries.1, s32[16,128]{1,0:T(8,128)} %bitcast.11, bf16[4,512,128]{2,1,0:T(8,128)(2,1)} %w_uv.1, bf16[512,7168]{1,0:T(8,128)(2,1)} %w_out.1, ...), custom_call_target="tpu_custom_call" | custom-call | tf_op jit(solution)/shard_map/layer/pallas_call | solution.py:549
  142.8 1.6 %copy.15 = bf16[8,7168]{1,0:T(8,128)(2,1)} copy(bf16[8,7168]{1,0:T(8,128)(2,1)} %layer.1) | data formatting | bytes 229376

commit v5 on v4

--- a/solution.py
+++ b/solution.py
@@ -342,13 +342,13 @@
     swap.start()
 
     def dispatch(side, k, dz):
-        to = on_ep(offset_of(k), dz)
+        to = on_ep(offset_of(k) + dz, dz)
         return copy_to(
             outgoing.at[side, to], arrived.at[side, e], t_send.at[side, k, dz], t_recv.at[side, k, dz], (s, to)
         )
 
     def give_back(k, dz):
-        to = on_ep(4 - offset_of(k), dz)
+        to = on_ep(4 - offset_of(k) + dz, dz)
         return copy_to(y_part.at[k, lax.rem(z + dz, 4)], returned.at[e], b_send.at[k, dz], b_recv.at[k, dz], (s, to))
 
     def gather(k, kind):
@@ -379,18 +379,16 @@
         ).astype(jnp.bfloat16).reshape(16, 16, 1792)
         arrived[side, e] = outgoing[side, e]
 
-    def send_rows(side, k):
-        for dz in (0, 1, 3, 2):
-            if k or dz:
-                dispatch(side, k, dz).start()
+    def send_rows(side, k, own=False):
+        for dz in (2, 1, 3) if own else (2, 1, 3, 0):
+            dispatch(side, k, dz).start()
 
     spread_rows(0)
-    send_rows(0, 0)
+    send_rows(0, 0, True)
     send_rows(0, 1)
     swap.wait_recv()
     spread_rows(1)
-    for side, k in ((1, 0), (0, 2), (1, 1), (0, 3), (1, 2), (1, 3)):
-        send_rows(side, k)
+    send_rows(1, 0, True)
 
     rows16 = lax.broadcasted_iota(jnp.int32, (16, 64), 0)
     cols64 = lax.broadcasted_iota(jnp.int32, (16, 64), 1)
@@ -403,8 +401,9 @@
         def _():
             dispatch(side, k, 0).wait_recv()
 
-        line = lax.rem(y + 4 - offset_of(k), 4)
-        block = arrived[side, pl.ds(line * 4, 4)].reshape(64, 1792)
+        block = jnp.concatenate([
+            arrived[side, lax.rem(y - z + 8 - offset_of(k) + i, 4) * 4 + i] for i in range(4)
+        ], axis=0)
         low = pl.multiple_of(lax.rem(s + 4 * side, 8) * 16, 16)
         for q in range(4):
             take = (cols64 == (rows16 // 4) * 16 + q * 4 + rows16 % 4).astype(jnp.bfloat16)
@@ -467,6 +466,14 @@
         def _():
             enter(0, t)
 
+        @pl.when(t < 2)
+        def _():
+            send_rows(0, t + 2)
+
+        @pl.when(t < 3)
+        def _():
+            send_rows(1, t + 1)
+
         @pl.when(t == 1)
         def _():
             for load in get_in:
@@ -474,12 +481,9 @@
 
         @pl.when((t >= 1) & (t < 5))
         def _():
+            enter(1, t - 1)
+            pass_on(t - 1)
             hidden(t - 1)
-
-        @pl.when(t < 4)
-        def _():
-            enter(1, t)
-            pass_on(t)
 
         @pl.when(t == 2)
         def _():

time: 145 us -> 135 us (0.931)
  Pallas kernels: 143 us -> 133 us
    pallas_call x1, Pallas kernels: 139 us -> 129 us  [layer_call(): pl.pallas_call(layer_kernel, name='layer', out_shape=jax.ShapeDtypeStruct...]
where the time goes in v5:
time: 135 us; the launch traced here: 134 us
  Pallas kernels  133 us (99%)
  local copies, waits for them, and re-layouts  1.55 us (1%)
    pallas_call x1, Pallas kernels, layer_call(): pl.pallas_call(layer_kernel, name='layer', out_shape=jax.ShapeDtypeStruct...  129 us
    pallas_call x1, Pallas kernels, serve(): pl.pallas_call(serve_kernel, name='serve', out_shape=(jax.ShapeDtypeStruc...  3.57 us

profile of v5, /device:TPU:1, one launch (start us, length us, event | category | flops | bytes accessed | tf_op | source)
XLA Modules:
  0.0 134.4 jit_solution(2726400332390892396)
XLA Ops:
  0.0 3.6 %serve.1 = (bf16[8,144,128]{2,1,0:T(8,128)(2,1)}, bf16[8,4,144,128]{3,2,1,0:T(8,128)(2,1)}) custom-call(s32[256]{0:T(256)} %group_passages.1, s32[256]{0:T(256)} %passage_place.1, bf16[32,576,128]{2,1,0:T(8,128)(2,1)} %bitcast.7), custom_call_target="tpu_custom_call" | custom-call | tf_op jit(solution)/shard_map/serve/pallas_call | solution.py:632
  3.6 129.3 %layer.1 = bf16[8,7168]{1,0:T(8,128)(2,1)} custom-call(bf16[8,144,128]{2,1,0:T(8,128)(2,1)} %get-tuple-element.7.served, bf16[8,4,144,128]{3,2,1,0:T(8,128)(2,1)} %get-tuple-element.8.served_far, bf16[128,2304]{1,0:T(8,128)(2,1)} %queries.1, s32[16,128]{1,0:T(8,128)} %bitcast.11, bf16[4,512,128]{2,1,0:T(8,128)(2,1)} %w_uv.1, bf16[512,7168]{1,0:T(8,128)(2,1)} %w_out.1, ...), custom_call_target="tpu_custom_call" | custom-call | tf_op jit(solution)/shard_map/layer/pallas_call | solution.py:553
  132.9 1.6 %copy.15 = bf16[8,7168]{1,0:T(8,128)(2,1)} copy(bf16[8,7168]{1,0:T(8,128)(2,1)} %layer.1) | data formatting | bytes 229376

commit v6 on v5

--- a/solution.py
+++ b/solution.py
@@ -21,7 +21,7 @@
     served, served_far, queries, row_slots, w_uv, w_out, residual, ids, gates, w_gate, w_up, w_down,
     out,
     kv, heads, mask, top, total, acc, head_out, out_w, part, part_in, summed, summed_in, rows,
-    table, weigh, normed, outgoing, arrived, x_rows, in_w, down_w, pre, hid, y_part, returned, mix_out, mix_in,
+    table, weigh, places, normed, outgoing, arrived, x_rows, in_w, down_w, pre, hid, y_part, returned, mix_out, mix_in,
     x_send, x_recv, g_send, g_recv, r_send, r_recv, d_send, d_recv, w_sem,
     n_send, n_recv, t_send, t_recv, a_send, a_recv, h_send, h_recv, b_send, b_recv, m_send, m_recv,
 ):
@@ -59,13 +59,13 @@
     for load in [get_w] + get_in:
         load.start()
 
-    lane_row = lax.broadcasted_iota(jnp.int32, (8, 128), 1) % 8
-    repeat = (lax.broadcasted_iota(jnp.int32, (8, 128), 0) == lane_row).astype(jnp.float32)
+    lane_row = lax.broadcasted_iota(jnp.int32, (1, 128), 1) % 8
+    repeat = (lax.broadcasted_iota(jnp.int32, (8, 1), 0) == lane_row).astype(jnp.float32)
     wide_ids = jnp.dot(ids[...].astype(jnp.float32), repeat, preferred_element_type=jnp.float32)
     wide_gates = jnp.dot(
         gates[...], repeat, preferred_element_type=jnp.float32, precision=lax.Precision.HIGHEST
     )
-    pair = lax.broadcasted_iota(jnp.int32, (64, 128), 0)
+    pair = lax.broadcasted_iota(jnp.int32, (64, 1), 0)
     expert = (pair // 4).astype(jnp.float32)
     routed = jnp.zeros((64, 128), jnp.float32)
     gate = jnp.zeros((64, 128), jnp.float32)
@@ -73,8 +73,8 @@
         named = (wide_ids[i:i + 1] == expert).astype(jnp.float32)
         routed = routed + named
         gate = gate + named * wide_gates[i:i + 1]
-    before = lax.broadcasted_iota(jnp.int32, (128, 128), 0)
-    upto = lax.broadcasted_iota(jnp.int32, (128, 128), 1) % 8
+    before = lax.broadcasted_iota(jnp.int32, (128, 1), 0)
+    upto = lax.broadcasted_iota(jnp.int32, (1, 128), 1) % 8
     earlier = jnp.dot(
         routed.astype(jnp.bfloat16), (before < upto).astype(jnp.bfloat16), preferred_element_type=jnp.float32
     )
@@ -122,15 +122,25 @@
                 for copy in far_copies(whole):
                     act(copy)
 
+    tables = []
+    for d in range(1, 8):
+        copy = pltpu.make_async_remote_copy(
+            src_ref=table.at[s], dst_ref=table.at[s], send_sem=n_send.at[d], recv_sem=n_recv.at[d],
+            device_id=at_s(d), device_id_type=MESH,
+        )
+        copy.start()
+        tables.append(copy)
+    each_far(lambda copy: copy.start())
+
     for h in range(4):
         heads[h * 128:(h + 1) * 128] = queries[:, h * 576:(h + 1) * 576]
-    slot = lax.broadcasted_iota(jnp.int32, (32, 128), 0)
+    slot = lax.broadcasted_iota(jnp.int32, (32, 1), 0)
     chosen = jnp.zeros((32, 128), jnp.bool_)
     for i in range(16):
         chosen = chosen | (row_slots[i:i + 1] == slot)
     chosen = chosen.astype(jnp.bfloat16)
-    slot_row = lax.broadcasted_iota(jnp.int32, (32, 512), 0)
-    token_col = lax.broadcasted_iota(jnp.int32, (32, 512), 1)
+    slot_row = lax.broadcasted_iota(jnp.int32, (32, 1), 0)
+    token_col = lax.broadcasted_iota(jnp.int32, (1, 512), 1)
     for j in range(4):
         for half in (0, 1):
             spread = (slot_row == (token_col // 128 + 4 * half) * 4 + j).astype(jnp.bfloat16)
@@ -162,10 +172,10 @@
         )
 
     def build_weigh():
-        lane = lax.broadcasted_iota(jnp.int32, (64, 128), 1)
+        lane = lax.broadcasted_iota(jnp.int32, (1, 128), 1)
         gated = jnp.concatenate([jnp.where(lane // 8 == g, table[g], 0.0) for g in range(8)], axis=0)
-        from_row = lax.broadcasted_iota(jnp.int32, (512, 512), 0)
-        to_col = lax.broadcasted_iota(jnp.int32, (512, 512), 1)
+        from_row = lax.broadcasted_iota(jnp.int32, (512, 1), 0)
+        to_col = lax.broadcasted_iota(jnp.int32, (1, 512), 1)
         place = (to_col // 4 % 8) * 64 + (to_col // 32) * 4 + to_col % 4
         move = (from_row == place).astype(jnp.bfloat16)
         high = gated.astype(jnp.bfloat16)
@@ -175,6 +185,17 @@
                 held, move, (((0,), (0,)), ((), ())), preferred_element_type=jnp.float32
             )[0:64].astype(jnp.bfloat16)
 
+    def build_place(side):
+        group = lax.rem(s + 4 * side, 8)
+        to_row = lax.broadcasted_iota(jnp.int32, (256, 1), 0)
+        from_pair = lax.broadcasted_iota(jnp.int32, (1, 64), 1)
+        widen = (from_pair == (to_row // 16) * 4 + to_row % 4).astype(jnp.bfloat16)
+        held = jnp.dot(
+            widen, (table[group] > 0).astype(jnp.bfloat16), preferred_element_type=jnp.float32
+        )[:, 0:32]
+        row_quarter = lax.broadcasted_iota(jnp.int32, (256, 1), 0) // 4 % 4
+        col_quarter = lax.broadcasted_iota(jnp.int32, (1, 32), 1) // 8
+        places[side] = jnp.where(row_quarter == col_quarter, held, 0.0).astype(jnp.bfloat16)
     def gather_copy(half, group, kind, place):
         low = half * 4 + (2 if kind == 3 else 0)
         size = 2 if kind >= 2 else 4
@@ -198,15 +219,6 @@
         copy.wait_recv()
     launch(None, 0)
     launch(0, 0)
-    tables = []
-    for d in range(1, 8):
-        copy = pltpu.make_async_remote_copy(
-            src_ref=table.at[s], dst_ref=table.at[s], send_sem=n_send.at[d], recv_sem=n_recv.at[d],
-            device_id=at_s(d), device_id_type=MESH,
-        )
-        copy.start()
-        tables.append(copy)
-    each_far(lambda copy: copy.start())
     keep_w = pltpu.make_async_copy(
         w_down.at[:, pl.ds(pl.multiple_of(s * 896, 896), 896)],
         down_w.at[pl.ds(pl.multiple_of(s * 256, 256), 256)], w_sem.at[1],
@@ -221,21 +233,20 @@
             send_sem=d_send.at[d - 1], recv_sem=d_recv.at[d - 1],
             device_id=to, device_id_type=MESH,
         )
-        copy.start()
+        if d != 4:
+            copy.start()
         moved.append(copy)
     for kind in (0, 1):
         offset = 1 if kind == 0 else 3
         for half in (0, 1):
             gather_copy(half, None, kind, (y, z)).wait_recv()
             gather_copy(half, None, kind + 2, chunk(half, offset, 0)).start()
-        launch(kind + 1, offset)
+    launch(1, 1)
+    launch(2, 3)
     for half in (0, 1):
         for kind in (2, 3):
             gather_copy(half, None, kind, (y, z)).wait_recv()
     launch(3, 2)
-    for copy in tables:
-        copy.wait_recv()
-    build_weigh()
     attend(y, 1)
 
     def take_far(copy):
@@ -298,6 +309,10 @@
             )
             copy.start()
             first.append(copy)
+    for copy in tables:
+        copy.wait_recv()
+    build_place(0)
+    build_place(1)
     second = []
     for half in (0, 1):
         for d in (1, 2, 3):
@@ -340,6 +355,7 @@
 
     swap = copy_to(normed.at[0], normed.at[1], n_send.at[0], n_recv.at[0], at_s(4))
     swap.start()
+    moved[3].start()
 
     def dispatch(side, k, dz):
         to = on_ep(offset_of(k) + dz, dz)
@@ -364,18 +380,8 @@
         return copy_to(ref, ref, h_send.at[k, kind], h_recv.at[k, kind], to)
 
     def spread_rows(side):
-        group = lax.rem(s + 4 * side, 8)
-        to_row = lax.broadcasted_iota(jnp.int32, (256, 64), 0)
-        from_pair = lax.broadcasted_iota(jnp.int32, (256, 64), 1)
-        widen = (from_pair == (to_row // 16) * 4 + to_row % 4).astype(jnp.bfloat16)
-        held = jnp.dot(
-            widen, (table[group] > 0).astype(jnp.bfloat16), preferred_element_type=jnp.float32
-        )[:, 0:32]
-        row_quarter = lax.broadcasted_iota(jnp.int32, (256, 32), 0) // 4 % 4
-        col_quarter = lax.broadcasted_iota(jnp.int32, (256, 32), 1) // 8
-        place = jnp.where(row_quarter == col_quarter, held, 0.0).astype(jnp.bfloat16)
         outgoing[side] = jnp.dot(
-            place, normed[side], preferred_element_type=jnp.float32
+            places[side], normed[side], preferred_element_type=jnp.float32
         ).astype(jnp.bfloat16).reshape(16, 16, 1792)
         arrived[side, e] = outgoing[side, e]
 
@@ -390,8 +396,8 @@
     spread_rows(1)
     send_rows(1, 0, True)
 
-    rows16 = lax.broadcasted_iota(jnp.int32, (16, 64), 0)
-    cols64 = lax.broadcasted_iota(jnp.int32, (16, 64), 1)
+    rows16 = lax.broadcasted_iota(jnp.int32, (16, 1), 0)
+    cols64 = lax.broadcasted_iota(jnp.int32, (1, 64), 1)
 
     def enter(side, k):
         for dz in range(1, 4):
@@ -438,8 +444,8 @@
         for kind in range(4):
             share(k, kind).start()
 
-    to128 = lax.broadcasted_iota(jnp.int32, (128, 128), 0)
-    from128 = lax.broadcasted_iota(jnp.int32, (128, 128), 1)
+    to128 = lax.broadcasted_iota(jnp.int32, (128, 1), 0)
+    from128 = lax.broadcasted_iota(jnp.int32, (1, 128), 1)
 
     def project(k):
         for kind in range(3):
@@ -473,6 +479,10 @@
         @pl.when(t < 3)
         def _():
             send_rows(1, t + 1)
+
+        @pl.when(t == 0)
+        def _():
+            build_weigh()
 
         @pl.when(t == 1)
         def _():
@@ -572,6 +582,7 @@
             pltpu.VMEM((4, 8, 1792), f32),
             pltpu.VMEM((8, 64, 128), f32),
             pltpu.VMEM((2, 64, 512), bf16),
+            pltpu.VMEM((2, 256, 32), bf16),
             pltpu.VMEM((2, 32, 1792), bf16),
             pltpu.VMEM((2, 16, 16, 1792), bf16),
             pltpu.VMEM((2, 16, 16, 1792), bf16),

time: 135 us -> 134 us (level)
  no operation moved by 1% of the time
where the time goes in v6:
time: 134 us
  Pallas kernels  133 us (99%)
  local copies, waits for them, and re-layouts  1.55 us (1%)
    pallas_call x1, Pallas kernels, layer_call(): pl.pallas_call(layer_kernel, name='layer', out_shape=jax.ShapeDtypeStruct...  129 us
    pallas_call x1, Pallas kernels, serve(): pl.pallas_call(serve_kernel, name='serve', out_shape=(jax.ShapeDtypeStruc...  3.6 us

profile of v6, /device:TPU:1, one launch (start us, length us, event | category | flops | bytes accessed | tf_op | source)
XLA Modules:
  0.0 134.5 jit_solution(5719422883050415965)
XLA Ops:
  0.0 3.6 %serve.1 = (bf16[8,144,128]{2,1,0:T(8,128)(2,1)}, bf16[8,4,144,128]{3,2,1,0:T(8,128)(2,1)}) custom-call(s32[256]{0:T(256)} %group_passages.1, s32[256]{0:T(256)} %passage_place.1, bf16[32,576,128]{2,1,0:T(8,128)(2,1)} %bitcast.7), custom_call_target="tpu_custom_call" | custom-call | tf_op jit(solution)/shard_map/serve/pallas_call | solution.py:643
  3.6 129.3 %layer.1 = bf16[8,7168]{1,0:T(8,128)(2,1)} custom-call(bf16[8,144,128]{2,1,0:T(8,128)(2,1)} %get-tuple-element.7.served, bf16[8,4,144,128]{3,2,1,0:T(8,128)(2,1)} %get-tuple-element.8.served_far, bf16[128,2304]{1,0:T(8,128)(2,1)} %queries.1, s32[16,128]{1,0:T(8,128)} %bitcast.11, bf16[4,512,128]{2,1,0:T(8,128)(2,1)} %w_uv.1, bf16[512,7168]{1,0:T(8,128)(2,1)} %w_out.1, ...), custom_call_target="tpu_custom_call" | custom-call | tf_op jit(solution)/shard_map/layer/pallas_call | solution.py:563
  132.9 1.6 %copy.15 = bf16[8,7168]{1,0:T(8,128)(2,1)} copy(bf16[8,7168]{1,0:T(8,128)(2,1)} %layer.1) | data formatting | bytes 229376

commit v7 on v6

--- a/solution.py
+++ b/solution.py
@@ -21,7 +21,7 @@
     served, served_far, queries, row_slots, w_uv, w_out, residual, ids, gates, w_gate, w_up, w_down,
     out,
     kv, heads, mask, top, total, acc, head_out, out_w, part, part_in, summed, summed_in, rows,
-    table, weigh, places, normed, outgoing, arrived, x_rows, in_w, down_w, pre, hid, y_part, returned, mix_out, mix_in,
+    raw, weights, shrink, table, weigh, places, normed, outgoing, arrived, x_rows, in_w, down_w, pre, hid, y_part, returned, mix_out, mix_in,
     x_send, x_recv, g_send, g_recv, r_send, r_recv, d_send, d_recv, w_sem,
     n_send, n_recv, t_send, t_recv, a_send, a_recv, h_send, h_recv, b_send, b_recv, m_send, m_recv,
 ):
@@ -158,17 +158,20 @@
 
     def attend(j, half):
         keys = jnp.concatenate([kv[j, half * 4 + i] for i in range(4)], axis=1)
-        scores = jnp.dot(heads[...], keys, preferred_element_type=jnp.float32) * SCALE
-        scores = (scores.reshape(4, 128, 512) + mask[j, half]).reshape(512, 512)
-        old = top[...]
-        new = jnp.maximum(old, jnp.max(scores, axis=1, keepdims=True))
-        exponent = jnp.exp2(scores - new[:, 0:1])
-        scale = jnp.exp2(old - new)
-        top[...] = new
-        total[...] = total[...] * scale + jnp.sum(exponent, axis=1, keepdims=True)
-        acc[...] = acc[...] * scale[:, 0:1] + lax.dot_general(
-            exponent.astype(jnp.bfloat16), keys[0:512], (((1,), (1,)), ((), ())),
-            preferred_element_type=jnp.float32,
+        raw[...] = jnp.dot(heads[...], keys, preferred_element_type=jnp.float32)
+        for low in range(0, 512, 64):
+            own = slice(low, low + 64)
+            scores = raw[own] * SCALE + mask[j, half, low % 128:low % 128 + 64]
+            old = top[own]
+            new = jnp.maximum(old, jnp.max(scores, axis=1, keepdims=True))
+            exponent = jnp.exp2(scores - new[:, 0:1])
+            scale = jnp.exp2(old - new)
+            top[own] = new
+            total[own] = total[own] * scale + jnp.sum(exponent, axis=1, keepdims=True)
+            shrink[own] = scale
+            weights[own] = exponent.astype(jnp.bfloat16)
+        acc[...] = acc[...] * shrink[:, 0:1] + lax.dot_general(
+            weights[...], keys[0:512], (((1,), (1,)), ((), ())), preferred_element_type=jnp.float32
         )
 
     def build_weigh():
@@ -395,6 +398,8 @@
     swap.wait_recv()
     spread_rows(1)
     send_rows(1, 0, True)
+    for side, k in ((0, 2), (1, 1), (0, 3), (1, 2), (1, 3)):
+        send_rows(side, k)
 
     rows16 = lax.broadcasted_iota(jnp.int32, (16, 1), 0)
     cols64 = lax.broadcasted_iota(jnp.int32, (1, 64), 1)
@@ -471,14 +476,6 @@
         @pl.when(t < 4)
         def _():
             enter(0, t)
-
-        @pl.when(t < 2)
-        def _():
-            send_rows(0, t + 2)
-
-        @pl.when(t < 3)
-        def _():
-            send_rows(1, t + 1)
 
         @pl.when(t == 0)
         def _():
@@ -580,6 +577,9 @@
             pltpu.VMEM((2, 4, 16, 1792), bf16),
             pltpu.VMEM((2, 3, 16, 1792), bf16),
             pltpu.VMEM((4, 8, 1792), f32),
+            pltpu.VMEM((512, 512), f32),
+            pltpu.VMEM((512, 512), bf16),
+            pltpu.VMEM((512, 128), f32),
             pltpu.VMEM((8, 64, 128), f32),
             pltpu.VMEM((2, 64, 512), bf16),
             pltpu.VMEM((2, 256, 32), bf16),

time: 134 us -> 134 us (level)
  no operation moved by 1% of the time
where the time goes in v7:
time: 134 us
  Pallas kernels  132 us (99%)
  local copies, waits for them, and re-layouts  1.55 us (1%)
    pallas_call x1, Pallas kernels, layer_call(): pl.pallas_call(layer_kernel, name='layer', out_shape=jax.ShapeDtypeStruct...  129 us
    pallas_call x1, Pallas kernels, serve(): pl.pallas_call(serve_kernel, name='serve', out_shape=(jax.ShapeDtypeStruc...  3.63 us

profile of v7, /device:TPU:1, one launch (start us, length us, event | category | flops | bytes accessed | tf_op | source)
XLA Modules:
  0.0 133.8 jit_solution(11264742282617499041)
XLA Ops:
  0.0 3.6 %serve.1 = (bf16[8,144,128]{2,1,0:T(8,128)(2,1)}, bf16[8,4,144,128]{3,2,1,0:T(8,128)(2,1)}) custom-call(s32[256]{0:T(256)} %group_passages.1, s32[256]{0:T(256)} %passage_place.1, bf16[32,576,128]{2,1,0:T(8,128)(2,1)} %bitcast.7), custom_call_target="tpu_custom_call" | custom-call | tf_op jit(solution)/shard_map/serve/pallas_call | solution.py:643
  3.6 128.6 %layer.1 = bf16[8,7168]{1,0:T(8,128)(2,1)} custom-call(bf16[8,144,128]{2,1,0:T(8,128)(2,1)} %get-tuple-element.7.served, bf16[8,4,144,128]{3,2,1,0:T(8,128)(2,1)} %get-tuple-element.8.served_far, bf16[128,2304]{1,0:T(8,128)(2,1)} %queries.1, s32[16,128]{1,0:T(8,128)} %bitcast.11, bf16[4,512,128]{2,1,0:T(8,128)(2,1)} %w_uv.1, bf16[512,7168]{1,0:T(8,128)(2,1)} %w_out.1, ...), custom_call_target="tpu_custom_call" | custom-call | tf_op jit(solution)/shard_map/layer/pallas_call | solution.py:560
  132.3 1.6 %copy.15 = bf16[8,7168]{1,0:T(8,128)(2,1)} copy(bf16[8,7168]{1,0:T(8,128)(2,1)} %layer.1) | data formatting | bytes 229376
